TPU v7x, 256 devices: a whole 4x4x8 slice. The times are simulated.
256 devices in a mesh: blk: 8 (over y_lo, x), grp: 32 (over z, y_hi, core).
Axes of the slice: x: 4, y: 4 (y_hi: 2, y_lo: 2; y = y_hi * 2 + y_lo), z: 8, core: 2. Of those that a mesh axis runs over, the one named last changes fastest.
Arguments:
- prefix: bfloat16 [8192, 4096], P('blk'), may hold values from -6 to 6
- latent: bfloat16 [2048, 4096], P(('blk', 'grp')), may hold values from -2.1 to 2.1
- limits: int32 [2048], P('blk'), may hold values from 1 to 8192, as said below
- gain_prefix: float32 [4096], replicated, may hold values from 0.1 to 1.9
- gain_latent: float32 [4096], replicated, may hold values from 0.1 to 1.9
- gain_state: float32 [4096], replicated, may hold values from 0.1 to 1.9
- cross_q: bfloat16 [4096, 4096], P('blk', 'grp'), may hold values from -4 to 4
- cross_k: bfloat16 [4096, 4096], P('blk', 'grp'), may hold values from -1 to 1
- cross_v: bfloat16 [4096, 4096], P('blk', 'grp'), may hold values from -0.09375 to 0.09375
- cross_o: bfloat16 [4096, 4096], P('grp', 'blk'), may hold values from -0.09375 to 0.09375
- delta_q: bfloat16 [4096, 4096], P('blk', 'grp'), may hold values from -0.046875 to 0.046875
- delta_k: bfloat16 [4096, 4096], P('blk', 'grp'), may hold values from -0.046875 to 0.046875
- delta_v: bfloat16 [4096, 4096], P('blk', 'grp'), may hold values from -0.046875 to 0.046875
- delta_o: bfloat16 [4096, 4096], P('grp', 'blk'), may hold values from -0.046875 to 0.046875
- self_q: bfloat16 [4096, 4096], P('blk', 'grp'), may hold values from -4 to 4
- self_k: bfloat16 [4096, 4096], P('blk', 'grp'), may hold values from -1 to 1
- self_v: bfloat16 [4096, 4096], P('blk', 'grp'), may hold values from -0.09375 to 0.09375
- self_o: bfloat16 [4096, 4096], P('grp', 'blk'), may hold values from -0.09375 to 0.09375
Outputs:
- latent_out: float32 [2048, 4096], P(('blk', 'grp'))
Inputs may be any that keep to these rules, and one draw needn't show every extreme that they name: `limits`: the value of latent row i is at least i * 4 + 1; the last equals 8192.
All inputs are finite; a program needn't handle non-finite values.
Results may differ from a plain program's by a relative error of at most 0.019.
Values may be sent and summed in bfloat16 or wider, within the bound.
A program may use at most 128 MiB of HBM per device.

v0:
```python
import jax
import jax.numpy as jnp
from jax import lax
from jax.sharding import PartitionSpec as P

HD = 128


epsilon = 1e-05
lowest_score = -1e30


def passed_along(block, axis, distance):
    devices = range(lax.axis_size(axis))
    route = [((i - distance) % len(devices), i) for i in devices]
    return lax.ppermute(block, axis, route)


def rms_scale(rows_in, gain):
    values = rows_in.astype(jnp.float32)
    inverse = lax.rsqrt(jnp.mean(values * values, axis=-1, keepdims=True) + epsilon)
    return (values * inverse * gain).astype(jnp.bfloat16)


def perturbed(weight, delta):
    return (weight.astype(jnp.float32) + delta.astype(jnp.float32)).astype(jnp.bfloat16)


def absorb(running, queries, key_block, allowed, col_width):
    row_max, row_total, weighted = running
    key_count = key_block.shape[0]
    heads_here = col_width // HD
    key_part = key_block[:, :col_width].reshape(key_count, heads_here, HD)
    value_part = key_block[:, col_width:].reshape(key_count, heads_here, HD)
    scores = jnp.einsum(
        "qhd,khd->qhk", queries, key_part, preferred_element_type=jnp.float32
    ) * HD ** (-0.5)
    scores = jnp.where(allowed[:, None, :], scores, lowest_score)
    new_max = jnp.maximum(row_max, jnp.max(scores, axis=2))
    exponent = jnp.where(allowed[:, None, :], jnp.exp(scores - new_max[:, :, None]), 0.0)
    factor = jnp.exp(row_max - new_max)
    row_total = row_total * factor + jnp.sum(exponent, axis=2)
    weighted = weighted * factor[:, :, None] + jnp.einsum(
        "qhk,khd->qhd",
        exponent,
        value_part.astype(jnp.float32),
        precision=lax.Precision.HIGHEST,
        preferred_element_type=jnp.float32,
    )
    return (new_max, row_total, weighted)


def finish(running):
    row_max, row_total, weighted = running
    return (weighted / row_total[:, :, None]).astype(jnp.bfloat16).reshape(weighted.shape[0], -1)


def shards(
    prefix,
    latent,
    limits,
    gain_prefix,
    gain_latent,
    gain_state,
    cross_q,
    cross_k,
    cross_v,
    cross_o,
    delta_q,
    delta_k,
    delta_v,
    delta_o,
    self_q,
    self_k,
    self_v,
    self_o,
):
    blocks = lax.axis_size("blk")
    groups = lax.axis_size("grp")
    blk_index = lax.axis_index("blk")
    grp_index = lax.axis_index("grp")
    gathered = (
        lax.all_gather(perturbed(cross_q, delta_q), "blk", axis=0, tiled=True),
        lax.all_gather(perturbed(cross_k, delta_k), "blk", axis=0, tiled=True),
        lax.all_gather(perturbed(cross_v, delta_v), "blk", axis=0, tiled=True),
        lax.all_gather(perturbed(cross_o, delta_o), "blk", axis=1, tiled=True),
        lax.all_gather(self_q, "blk", axis=0, tiled=True),
        lax.all_gather(self_k, "blk", axis=0, tiled=True),
        lax.all_gather(self_v, "blk", axis=0, tiled=True),
        lax.all_gather(self_o, "blk", axis=1, tiled=True),
    )
    w_query, w_key, w_value, w_out, s_query, s_key, s_value, s_out = gathered
    col_width = w_query.shape[1]
    heads_here = col_width // HD
    latent_all = lax.all_gather(latent, "grp", axis=0, tiled=True)
    latent_rows = latent_all.shape[0]
    prefix_rows = prefix.shape[0]
    row_share = latent_rows // groups
    row_ids = blk_index * latent_rows + jnp.arange(latent_rows, dtype=jnp.int32)
    w_keyval = jnp.concatenate([w_key, w_value], axis=1)
    latent_n = rms_scale(latent_all, gain_latent)
    queries = (
        jnp.dot(latent_n, w_query, preferred_element_type=jnp.float32)
        .astype(jnp.bfloat16)
        .reshape(latent_rows, heads_here, HD)
    )
    latent_kv = jnp.dot(latent_n, w_keyval, preferred_element_type=jnp.float32).astype(jnp.bfloat16)
    prefix_kv = jnp.dot(
        rms_scale(prefix, gain_prefix), w_keyval, preferred_element_type=jnp.float32
    ).astype(jnp.bfloat16)
    own_block = jnp.concatenate([prefix_kv, latent_kv], axis=0)

    def prefix_part(running, key_block, source):
        key_ids = source * prefix_rows + jnp.arange(prefix_rows, dtype=jnp.int32)
        allowed = key_ids[None, :] < limits[:, None]
        return absorb(running, queries, key_block[:prefix_rows], allowed, col_width)

    def latent_part(running, key_block, source):
        key_ids = source * latent_rows + jnp.arange(latent_rows, dtype=jnp.int32)
        allowed = key_ids[None, :] <= row_ids[:, None]
        return absorb(running, queries, key_block[prefix_rows:], allowed, col_width)

    def visit_block(running, key_block, source):
        return latent_part(prefix_part(running, key_block, source), key_block, source)

    start_state = (
        jnp.full((latent_rows, heads_here), lowest_score, jnp.float32),
        jnp.zeros((latent_rows, heads_here), jnp.float32),
        jnp.zeros((latent_rows, heads_here, HD), jnp.float32),
    )
    running = visit_block(start_state, own_block, blk_index)
    moving = own_block
    for offset in range(1, blocks):
        moving = passed_along(moving, "blk", 1)
        running = visit_block(running, moving, (blk_index - offset) % blocks)
    mixed_cross = finish(running)
    cross_total = lax.psum(jnp.dot(mixed_cross, w_out, preferred_element_type=jnp.float32), "grp")
    carried_all = latent_all.astype(jnp.float32) + cross_total
    carried_here = lax.dynamic_slice_in_dim(carried_all, grp_index * row_share, row_share, 0)
    carried_n = rms_scale(carried_all, gain_state)
    self_queries = (
        jnp.dot(carried_n, s_query, preferred_element_type=jnp.float32)
        .astype(jnp.bfloat16)
        .reshape(latent_rows, heads_here, HD)
    )
    self_kv = jnp.dot(
        carried_n, jnp.concatenate([s_key, s_value], axis=1), preferred_element_type=jnp.float32
    ).astype(jnp.bfloat16)
    key_piece = lax.all_gather(self_kv, "blk", axis=0, tiled=True)
    key_ids = jnp.arange(key_piece.shape[0], dtype=jnp.int32)
    allowed = key_ids[None, :] <= row_ids[:, None]
    self_state = absorb(start_state, self_queries, key_piece, allowed, col_width)
    mixed_self = finish(self_state)
    self_share = lax.psum_scatter(
        jnp.dot(mixed_self, s_out, preferred_element_type=jnp.float32).astype(jnp.bfloat16),
        "grp",
        scatter_dimension=0,
        tiled=True,
    ).astype(jnp.float32)
    return carried_here + self_share


def solution(mesh):
    return jax.shard_map(
        shards,
        mesh=mesh,
        in_specs=(
            P("blk", None),
            P(("blk", "grp"), None),
            P("blk"),
            P(),
            P(),
            P(),
            P("blk", "grp"),
            P("blk", "grp"),
            P("blk", "grp"),
            P("grp", "blk"),
            P("blk", "grp"),
            P("blk", "grp"),
            P("blk", "grp"),
            P("grp", "blk"),
            P("blk", "grp"),
            P("blk", "grp"),
            P("blk", "grp"),
            P("grp", "blk"),
        ),
        out_specs=P(("blk", "grp"), None),
        check_vma=False,
    )
```

profile of v0, /device:TPU:40, one launch (start us, length us, event | category | flops | bytes accessed | tf_op | source)
XLA Modules:
  0.0 957.3 jit_solution(9503003684826612811)
XLA Ops:
  6.5 1.7 add_convert_fusion.3
  8.3 1.7 add_convert_fusion.2
  10.0 0.7 all-gather.11.cloned.1.call-update
  10.7 1.7 add_convert_fusion.1
  12.5 1.6 add_convert_fusion
  14.3 5.1 fusion
  19.4 32.8 %all-gather.13.cloned.1.call-done = bf16[4096,128]{1,0:T(8,128)(2,1)} async-done(((bf16[512,128]{1,0:T(8,128)(2,1)}), bf16[4096,128]{1,0:T(8,128)(2,1)}) %all-gather.13.cloned.1.call-update) | async-done | bytes 1048592 | tf_op jit(solution)/shard_map/all_gather | solution.py:84
  52.2 1.4 constant_dynamic-update-slice_fusion.1
  53.6 40.9 %all-gather.15.cloned.1.call-done = bf16[4096,128]{1,0:T(8,128)(2,1)} async-done(((bf16[512,128]{1,0:T(8,128)(2,1)}), bf16[4096,128]{1,0:T(8,128)(2,1)}) %all-gather.15.cloned.1.call-update) | async-done | bytes 1048592 | tf_op jit(solution)/shard_map/all_gather | solution.py:85
  94.6 1.5 constant_dynamic-update-slice_fusion
  96.1 6.5 fusion.27
  102.6 73.0 %all-gather.11.cloned.1.call-done = bf16[256,4096]{1,0:T(8,128)(2,1)} async-done(((bf16[8,4096]{1,0:T(8,128)(2,1)}), bf16[256,4096]{1,0:T(8,128)(2,1)}) %all-gather.11.cloned.1.call-update) | async-done | bytes 2097168 | tf_op jit(solution)/shard_map/all_gather | solution.py:95
  175.7 2.2 fusion.7
  177.9 2.3 convolution_convert_fusion.1
  180.3 1.5 collective-permute-start
  181.9 23.8 %collective-permute-done = bf16[1280,256]{1,0:T(8,128)(2,1)S(1)} collective-permute-done((bf16[1280,256]{1,0:T(8,128)(2,1)S(1)}, bf16[1280,256]{1,0:T(8,128)(2,1)S(1)}, u32[]{:S(2)}, u32[]{:S(2)}) %collective-permute-start) | collective-permute-done | bytes 655392 | tf_op jit(solution)/shard_map/ppermute | solution.py:16
  205.8 19.7 %collective-permute-done.1 = bf16[1280,256]{1,0:T(8,128)(2,1)} collective-permute-done((bf16[1280,256]{1,0:T(8,128)(2,1)S(1)}, bf16[1280,256]{1,0:T(8,128)(2,1)}, u32[]{:S(2)}, u32[]{:S(2)}) %collective-permute-start.1) | collective-permute-done | bytes 655392 | tf_op jit(solution)/shard_map/ppermute | solution.py:16
  225.5 2.0 convolution_convert_fusion.3
  227.7 0.4 fusion.271
  228.1 21.8 %collective-permute-done.2 = bf16[1280,256]{1,0:T(8,128)(2,1)} collective-permute-done((bf16[1280,256]{1,0:T(8,128)(2,1)}, bf16[1280,256]{1,0:T(8,128)(2,1)}, u32[]{:S(2)}, u32[]{:S(2)}) %collective-permute-start.2) | collective-permute-done | bytes 655392 | tf_op jit(solution)/shard_map/ppermute | solution.py:16
  250.1 0.4 fusion.269
  250.5 1.3 fusion.267
  251.8 16.1 %collective-permute-done.3 = bf16[1280,256]{1,0:T(8,128)(2,1)S(1)} collective-permute-done((bf16[1280,256]{1,0:T(8,128)(2,1)}, bf16[1280,256]{1,0:T(8,128)(2,1)S(1)}, u32[]{:S(2)}, u32[]{:S(2)}) %collective-permute-start.3) | collective-permute-done | bytes 655392 | tf_op jit(solution)/shard_map/ppermute | solution.py:16
  267.9 1.1 fusion.266
  268.9 1.1 fusion.264
  270.0 1.3 fusion.265
  271.3 13.1 %collective-permute-done.4 = bf16[1280,256]{1,0:T(8,128)(2,1)S(1)} collective-permute-done((bf16[1280,256]{1,0:T(8,128)(2,1)S(1)}, bf16[1280,256]{1,0:T(8,128)(2,1)S(1)}, u32[]{:S(2)}, u32[]{:S(2)}) %collective-permute-start.4) | collective-permute-done | bytes 655392 | tf_op jit(solution)/shard_map/ppermute | solution.py:16
  284.6 0.4 fusion.263
  285.3 14.6 %collective-permute-done.5 = bf16[1280,256]{1,0:T(8,128)(2,1)S(1)} collective-permute-done((bf16[1280,256]{1,0:T(8,128)(2,1)S(1)}, bf16[1280,256]{1,0:T(8,128)(2,1)S(1)}, u32[]{:S(2)}, u32[]{:S(2)}) %collective-permute-start.5) | collective-permute-done | bytes 655392 | tf_op jit(solution)/shard_map/ppermute | solution.py:16
  300.4 0.4 fusion.259
  300.8 13.8 %collective-permute-done.6 = bf16[1280,256]{1,0:T(8,128)(2,1)S(1)} collective-permute-done((bf16[1280,256]{1,0:T(8,128)(2,1)S(1)}, bf16[1280,256]{1,0:T(8,128)(2,1)S(1)}, u32[]{:S(2)}, u32[]{:S(2)}) %collective-permute-start.6) | collective-permute-done | bytes 655392 | tf_op jit(solution)/shard_map/ppermute | solution.py:16
  315.6 0.7 fusion.116
  316.4 0.4 fusion.178
  316.8 1.7 fusion.110
  318.5 0.8 fusion.61
  319.7 1.2 convolution_bitcast_fusion.10
  320.9 1.2 convolution_bitcast_fusion.8
  323.5 0.8 fusion.65
  324.3 1.8 fusion.69
  326.0 1.8 fusion.74
  327.8 0.8 fusion.78
  328.6 0.8 fusion.82
  329.4 0.8 fusion.86
  330.3 0.8 fusion.98
  331.1 3.9 fusion.273
  335.1 0.7 all-gather.21.cloned.1.call-update
  335.8 0.7 all-gather.23.cloned.1.call-update
  336.6 0.7 all-gather.27.cloned.1.call-update
  337.6 270.7 %all-reduce.2.cloned.1.call-done = f32[256,4096]{1,0:T(8,128)} async-done(((f32[256,4096]{1,0:T(8,128)}), f32[256,4096]{1,0:T(8,128)}) %all-reduce.2.cloned.1.call-update) | async-done | bytes 4194320 | tf_op jit(solution)/shard_map/psum | solution.py:137
  608.3 4.6 multiply_reduce_fusion
  612.9 44.9 %all-gather.21.cloned.1.call-done = bf16[4096,128]{1,0:T(8,128)(2,1)} async-done(((bf16[512,128]{1,0:T(8,128)(2,1)}), bf16[4096,128]{1,0:T(8,128)(2,1)}) %all-gather.21.cloned.1.call-update) | async-done | bytes 1048592 | tf_op jit(solution)/shard_map/all_gather | solution.py:88
  657.8 42.4 %all-gather.23.cloned.1.call-done = bf16[4096,128]{1,0:T(8,128)(2,1)} async-done(((bf16[512,128]{1,0:T(8,128)(2,1)}), bf16[4096,128]{1,0:T(8,128)(2,1)}) %all-gather.23.cloned.1.call-update) | async-done | bytes 1048592 | tf_op jit(solution)/shard_map/all_gather | solution.py:89
  700.2 4.2 fusion.38
  704.5 0.7 all-gather.29.cloned.1.call-update
  705.2 37.4 %all-gather.27.cloned.1.call-done = bf16[4096,128]{1,0:T(8,128)(2,1)} async-done(((bf16[512,128]{1,0:T(8,128)(2,1)}), bf16[4096,128]{1,0:T(8,128)(2,1)}) %all-gather.27.cloned.1.call-update) | async-done | bytes 1048592 | tf_op jit(solution)/shard_map/all_gather | solution.py:87
  742.6 42.2 %all-gather.25.cloned.1.call-done = bf16[2048,256]{1,0:T(8,128)(2,1)} async-done(((bf16[256,256]{1,0:T(8,128)(2,1)}), bf16[2048,256]{1,0:T(8,128)(2,1)}) %all-gather.25.cloned.1.call-update) | async-done | bytes 1048592 | tf_op jit(solution)/shard_map/all_gather | solution.py:149
  784.8 3.9 fusion.272
  788.7 0.5 fusion.18
  789.3 0.7 copy-done.2
  789.9 1.4 fusion.95
  791.3 35.9 %all-gather.29.cloned.1.call-done = bf16[128,4096]{1,0:T(8,128)(2,1)} async-done(((bf16[128,512]{1,0:T(8,128)(2,1)}), bf16[128,4096]{1,0:T(8,128)(2,1)}) %all-gather.29.cloned.1.call-update) | async-done | bytes 1048592 | tf_op jit(solution)/shard_map/all_gather | solution.py:90
  827.2 3.3 convolution_convert_fusion
  830.5 118.4 %reduce-scatter.2.cloned.1.call-done = bf16[8,4096]{1,0:T(8,128)(2,1)} async-done(((bf16[256,4096]{1,0:T(8,128)(2,1)}), bf16[8,4096]{1,0:T(8,128)(2,1)}) %reduce-scatter.2.cloned.1.call-update) | async-done | bytes 65552 | tf_op jit(solution)/shard_map/reduce_scatter | solution.py:154
  948.9 1.6 convert_add_fusion.1
  (75 shorter events, 5.4 us)
Async XLA Ops:
  6.5 45.7 %all-gather.13.cloned.1.call-start = ((), (), s32[]{:S(2)}) async-start(), calls=%async_computation.2 | async-start | bytes 1179648 | tf_op jit(solution)/shard_map/all_gather | solution.py:84
  8.2 86.3 %all-gather.15.cloned.1.call-start = ((), (), s32[]{:S(2)}) async-start(), calls=%async_computation.3 | async-start | bytes 1179648 | tf_op jit(solution)/shard_map/all_gather | solution.py:85
  9.9 165.7 %all-gather.11.cloned.1.call-start = ((), (), s32[]{:S(2)}) async-start(), calls=%async_computation.1 | async-start | bytes 2162688 | tf_op jit(solution)/shard_map/all_gather | solution.py:95
  10.7 214.8 %all-gather.17.cloned.1.call-start = ((), (), s32[]{:S(2)}) async-start(), calls=%async_computation.4 | async-start | bytes 1179648 | tf_op jit(solution)/shard_map/all_gather | solution.py:83
  12.4 318.7 %all-gather.19.cloned.1.call-start = ((), (), s32[]{:S(2)}) async-start(), calls=%async_computation.5 | async-start | bytes 1179648 | tf_op jit(solution)/shard_map/all_gather | solution.py:86
  14.1 594.1 %all-reduce.2.cloned.1.call-start = ((), (), s32[]{:S(2)}) async-start(), calls=%async_computation.6 | async-start | bytes 8388608 | tf_op jit(solution)/shard_map/psum | solution.py:137
  19.4 76.7 %copy-start.5 = (f32[4096]{0:T(1024)S(1)}, f32[4096]{0:T(1024)}, u32[]{:S(2)}) copy-start(f32[4096]{0:T(1024)} %param.21) | copy-start | bytes 49156
  96.0 6.6 copy-start.1
  96.1 81.8 %copy-start.6 = (f32[4096]{0:T(1024)S(1)}, f32[4096]{0:T(1024)}, u32[]{:S(2)}) copy-start(f32[4096]{0:T(1024)} %param.22) | copy-start | bytes 49156
  175.6 2.3 copy-start
  180.3 25.4 %collective-permute-start = (bf16[1280,256]{1,0:T(8,128)(2,1)S(1)}, bf16[1280,256]{1,0:T(8,128)(2,1)S(1)}, u32[]{:S(2)}, u32[]{:S(2)}) collective-permute-start(bf16[1280,256]{1,0:T(8,128)(2,1)S(1)} %pad_maximum_fusion), channel_id=1, source_target_pairs={{224,0},{0,32},{32,64},{64,96},{96,128},{128,160},{160,192},{192,2... | collective-permute-start | bytes 1966088 | tf_op jit(solution)/shard_map/ppermute | solution.py:16
  205.7 19.7 %collective-permute-start.1 = (bf16[1280,256]{1,0:T(8,128)(2,1)S(1)}, bf16[1280,256]{1,0:T(8,128)(2,1)}, u32[]{:S(2)}, u32[]{:S(2)}) collective-permute-start(bf16[1280,256]{1,0:T(8,128)(2,1)S(1)} %collective-permute-done), channel_id=1, source_target_pairs={{224,0},{0,32},{32,64},{64,96},{96,128},{128,160},{160,192},{192,2... | collective-permute-start | bytes 1966088 | tf_op jit(solution)/shard_map/ppermute | solution.py:16
  205.8 22.0 %copy-start.4 = (s32[256]{0:T(256)S(1)}, s32[256]{0:T(256)}, u32[]{:S(2)}) copy-start(s32[256]{0:T(256)} %param.20) | copy-start | bytes 3076
  225.5 24.4 %collective-permute-start.2 = (bf16[1280,256]{1,0:T(8,128)(2,1)}, bf16[1280,256]{1,0:T(8,128)(2,1)}, u32[]{:S(2)}, u32[]{:S(2)}) collective-permute-start(bf16[1280,256]{1,0:T(8,128)(2,1)} %collective-permute-done.1), channel_id=1, source_target_pairs={{224,0},{0,32},{32,64},{64,96},{96,128},{128,160},{160,192},{192,2... | collective-permute-start | bytes 1966088 | tf_op jit(solution)/shard_map/ppermute | solution.py:16
  249.9 18.0 %collective-permute-start.3 = (bf16[1280,256]{1,0:T(8,128)(2,1)}, bf16[1280,256]{1,0:T(8,128)(2,1)S(1)}, u32[]{:S(2)}, u32[]{:S(2)}) collective-permute-start(bf16[1280,256]{1,0:T(8,128)(2,1)} %collective-permute-done.2), channel_id=1, source_target_pairs={{224,0},{0,32},{32,64},{64,96},{96,128},{128,160},{160,192},{192,2... | collective-permute-start | bytes 1966088 | tf_op jit(solution)/shard_map/ppermute | solution.py:16
  267.9 16.5 %collective-permute-start.4 = (bf16[1280,256]{1,0:T(8,128)(2,1)S(1)}, bf16[1280,256]{1,0:T(8,128)(2,1)S(1)}, u32[]{:S(2)}, u32[]{:S(2)}) collective-permute-start(bf16[1280,256]{1,0:T(8,128)(2,1)S(1)} %collective-permute-done.3), channel_id=1, source_target_pairs={{224,0},{0,32},{32,64},{64,96},{96,128},{128,160},{160,192},{192,2... | collective-permute-start | bytes 1966088 | tf_op jit(solution)/shard_map/ppermute | solution.py:16
  284.4 15.6 %collective-permute-start.5 = (bf16[1280,256]{1,0:T(8,128)(2,1)S(1)}, bf16[1280,256]{1,0:T(8,128)(2,1)S(1)}, u32[]{:S(2)}, u32[]{:S(2)}) collective-permute-start(bf16[1280,256]{1,0:T(8,128)(2,1)S(1)} %collective-permute-done.4), channel_id=1, source_target_pairs={{224,0},{0,32},{32,64},{64,96},{96,128},{128,160},{160,192},{192,2... | collective-permute-start | bytes 1966088 | tf_op jit(solution)/shard_map/ppermute | solution.py:16
  299.9 14.7 %collective-permute-start.6 = (bf16[1280,256]{1,0:T(8,128)(2,1)S(1)}, bf16[1280,256]{1,0:T(8,128)(2,1)S(1)}, u32[]{:S(2)}, u32[]{:S(2)}) collective-permute-start(bf16[1280,256]{1,0:T(8,128)(2,1)S(1)} %collective-permute-done.5), channel_id=1, source_target_pairs={{224,0},{0,32},{32,64},{64,96},{96,128},{128,160},{160,192},{192,2... | collective-permute-start | bytes 1966088 | tf_op jit(solution)/shard_map/ppermute | solution.py:16
  335.0 322.8 %all-gather.21.cloned.1.call-start = ((), (), s32[]{:S(2)}) async-start(), calls=%async_computation.7 | async-start | bytes 1179648 | tf_op jit(solution)/shard_map/all_gather | solution.py:88
  335.8 364.4 %all-gather.23.cloned.1.call-start = ((), (), s32[]{:S(2)}) async-start(), calls=%async_computation.8 | async-start | bytes 1179648 | tf_op jit(solution)/shard_map/all_gather | solution.py:89
  336.5 406.0 %all-gather.27.cloned.1.call-start = ((), (), s32[]{:S(2)}) async-start(), calls=%async_computation.10 | async-start | bytes 1179648 | tf_op jit(solution)/shard_map/all_gather | solution.py:87
  337.3 363.0 %copy-start.3 = (f32[4096]{0:T(1024)S(1)}, f32[4096]{0:T(1024)}, u32[]{:S(2)}) copy-start(f32[4096]{0:T(1024)} %param.23) | copy-start | bytes 49156
  337.3 447.5 %all-gather.25.cloned.1.call-start = ((), (), s32[]{:S(2)}) async-start(), calls=%async_computation.9 | async-start | bytes 1179648 | tf_op jit(solution)/shard_map/all_gather | solution.py:149
  704.4 122.7 %all-gather.29.cloned.1.call-start = ((), (), s32[]{:S(2)}) async-start(), calls=%async_computation.11 | async-start | bytes 1179648 | tf_op jit(solution)/shard_map/all_gather | solution.py:90
  705.2 243.7 %reduce-scatter.2.cloned.1.call-start = ((), (), s32[]{:S(2)}) async-start(), calls=%async_computation.12 | async-start | bytes 2162688 | tf_op jit(solution)/shard_map/reduce_scatter | solution.py:154
  788.7 1.2 copy-start.2
Sparse Core Ops, SparseCore 0:
  9.1 43.0 all-gather.12
  54.0 40.5 all-gather.14
  97.4 78.2 all-gather.10
  177.3 39.6 all-gather.16
  218.7 41.5 all-gather.18
  335.1 273.0 all-reduce.1
  610.1 47.7 all-gather.20
  659.6 40.5 all-gather.22
  702.0 40.5 all-gather.26
  744.2 40.5 all-gather.24
  786.6 40.5 all-gather.28
  831.2 117.6 reduce-scatter.1
where the time goes:
time: 960 us; the launch traced here: 957 us
  waiting for transfers between devices  865 us (90%)
  matrix products  48.6 us (5%)
  other arithmetic  23.9 us (2%)
  between operations  14.1 us (1%)
    psum x1, waiting for transfers between devices, shards(): lax.psum(jnp.dot(mixed_cross, w_out, preferred_element_type=jnp.float32),...  271 us
    ppermute x7, waiting for transfers between devices, passed_along(): return lax.ppermute(block, axis, route)  123 us
    reduce_scatter x1, waiting for transfers between devices, shards(): lax.psum_scatter(jnp.dot(mixed_self, s_out, preferred_element_type=jnp.fl...  118 us
    all_gather x1, waiting for transfers between devices, shards(): latent_all = lax.all_gather(latent, 'grp', axis=0, tiled=True)  73 us
    all_gather x1, waiting for transfers between devices, shards(): lax.all_gather(self_k, 'blk', axis=0, tiled=True)  44.9 us
    all_gather x1, waiting for transfers between devices, shards(): lax.all_gather(self_v, 'blk', axis=0, tiled=True)  42.4 us
    all_gather x1, waiting for transfers between devices, shards(): key_piece = lax.all_gather(self_kv, 'blk', axis=0, tiled=True)  42.2 us
    all_gather x1, waiting for transfers between devices, shards(): lax.all_gather(perturbed(cross_v, delta_v), 'blk', axis=0, tiled=True)  40.9 us
  transfers between devices with their start and end apart: 19, of which 17 were waited for; matrix products, arithmetic and copies ran while one was open for 7% of the time, Pallas kernels for 0%

commit v1 on v0

v1 whole, which is shorter than its diff:
```python
import functools

import jax
import jax.numpy as jnp
from jax import lax
from jax.experimental import pallas as pl
from jax.experimental.pallas import tpu as pltpu
from jax.sharding import PartitionSpec as P

D = 4096
HD = 128
HALF = D // 2
EPS = 1e-05
SCALE = HD ** (-0.5)
LOW = -1e30
CLIP = -1e20
MESH = pl.DeviceIdType.MESH
F32 = jnp.float32
BF16 = jnp.bfloat16

N_SEM = 0


def _places(count):
    global N_SEM
    first = N_SEM
    N_SEM += count
    return first


S_WQ = _places(8)
S_WKV = _places(8)
S_WO = _places(8)
S_SQKV = _places(8)
S_SO = _places(8)
S_LIM = _places(8)
S_Q = _places(8)
S_O = _places(8)
S_ST = _places(8)
S_K2 = _places(8)
S_V2 = _places(8)
S_AGY = _places(2)
S_AGZ = _places(2 * 2 * 5)
S_AGC = _places(2 * 8)
S_RSC = _places(2)
S_RSZ = _places(2 * 2 * 2 * 5)
S_RSY = _places(2)


def rms_rows(values, gain):
    inverse = lax.rsqrt(jnp.sum(values * values, axis=1, keepdims=True) * (1.0 / D) + EPS)
    return values * inverse * gain


def pack_rows(rows):
    return jnp.concatenate([rows[:, :HALF], rows[:, HALF:]], axis=0)


def unpack_rows(packed):
    return jnp.concatenate([packed[:8], packed[8:]], axis=1)


def dot(a, b, ca=1, cb=0):
    return lax.dot_general(a, b, (((ca,), (cb,)), ((), ())), preferred_element_type=F32)


def layer_kernel(
    prefix, latent, limits, gain_p, gain_l, gain_s,
    cq, ck, cv, co, dq, dk, dv, do, sq, sk, sv, so_in,
    out,
    pre, wq, wkv, wo, sqkv, so, lim, qn, kn, vt, acc, qacc, scores,
    otx, orx, sttx, strx, mixed, k2, v2, o2,
    pk, pkr, gat, part, sib, rtx, rrx, ytx, yrx, carried,
    ss, rs, ls,
):
    b = lax.axis_index("blk")
    g = lax.axis_index("grp")
    x, yl = b % 4, b // 4
    z, yh, c = g // 4, (g // 2) % 2, g % 2

    def blk_to(i):
        return {"blk": ((yl + i // 4) % 2) * 4 + (x + i % 4) % 4, "grp": g}

    def blk_from(i):
        return ((yl + i // 4) % 2) * 4 + (x + 4 - i % 4) % 4

    def grp_at(zz, yy, cc):
        return {"blk": b, "grp": (zz * 2 + yy) * 2 + cc}

    sibling = grp_at(z, yh, 1 - c)
    across = grp_at(z, 1 - yh, c)
    above = grp_at((z + 1) % 8, yh, c)
    below = grp_at((z + 7) % 8, yh, c)
    vertical = (above, below)

    def remote(src, dst, place, device):
        return pltpu.make_async_remote_copy(
            src_ref=src, dst_ref=dst, send_sem=ss.at[place], recv_sem=rs.at[place],
            device_id=device, device_id_type=MESH,
        )

    sent = []

    def send(src, dst, place, device):
        copy = remote(src, dst, place, device)
        copy.start()
        sent.append(copy)

    def arrived(dst, place):
        remote(dst, dst, place, sibling).wait_recv()

    barrier = pltpu.get_barrier_semaphore()
    for i in range(1, 8):
        pl.semaphore_signal(barrier, inc=1, device_id=blk_to(i), device_id_type=MESH)
    for device in (sibling, across, above, below):
        pl.semaphore_signal(barrier, inc=1, device_id=device, device_id_type=MESH)

    loads = [
        pltpu.make_async_copy(prefix.at[pl.ds(t * 256, 256)], pre.at[pl.ds(t * 256, 256)], ls.at[t])
        for t in range(4)
    ]
    for load in loads:
        load.start()

    def perturbed(weight, delta):
        return (weight[...].astype(F32) + delta[...].astype(F32)).astype(BF16)

    rows_l = rms_rows(latent[...].astype(F32), gain_l[...])
    pk[0] = pack_rows(rows_l).astype(BF16)
    lim[0] = jnp.broadcast_to(limits[...], (8, 256))
    wq[0] = perturbed(cq, dq)
    wkv[0, :, :HD] = perturbed(ck, dk)
    wkv[0, :, HD:] = perturbed(cv, dv)
    pl.semaphore_wait(barrier, 11)

    def gather_begin(u):
        send(pk.at[u], pkr.at[u], S_AGY + u, across)

    def gather_pair(u, rows):
        arrived(pkr.at[u], S_AGY + u)
        other = unpack_rows(pkr[u].astype(F32))
        low = jnp.where(yh == 0, rows, other)
        high = jnp.where(yh == 0, other, rows)
        gat[u, z, c] = jnp.concatenate([low, high], axis=0).astype(BF16)
        own = gat.at[u, z, c]
        for way in range(2):
            send(own, own, S_AGZ + (u * 2 + way) * 5 + 1, vertical[way])
        send(own, own, S_AGC + u * 8, sibling)

    def gather_step(u, k):
        for way in range(2):
            zz = (z + 8 - k) % 8 if way == 0 else (z + k) % 8
            chunk = gat.at[u, zz, c]
            if k < 4:
                arrived(chunk, S_AGZ + (u * 2 + way) * 5 + k)
                onward = chunk
                if k == 3:
                    onward = gat.at[u, zz, c, :, pl.ds(way * HALF, HALF)]
                send(onward, onward, S_AGZ + (u * 2 + way) * 5 + k + 1, vertical[way])
                send(chunk, chunk, S_AGC + u * 8 + (k if way == 0 else 8 - k), sibling)
            else:
                piece = gat.at[u, zz, c, :, pl.ds(way * HALF, HALF)]
                arrived(piece, S_AGZ + (u * 2 + way) * 5 + 4)
        if k == 4:
            chunk = gat.at[u, (z + 4) % 8, c]
            send(chunk, chunk, S_AGC + u * 8 + 4, sibling)

    def gather_end(u):
        for k in range(8):
            arrived(gat.at[u, (z + 8 - k) % 8, 1 - c], S_AGC + u * 8 + k)

    gather_begin(0)
    for i in range(1, 8):
        send(lim.at[0], lim.at[i], S_LIM + i, blk_to(i))
    for i in range(1, 8):
        send(wq.at[0], wq.at[i], S_WQ + i, blk_to(i))
    for i in range(1, 8):
        send(wkv.at[0], wkv.at[i], S_WKV + i, blk_to(i))
    gather_pair(0, rows_l)

    def norm_prefix(t):
        loads[t].wait()

        def tile(n, carry):
            rows = pl.ds(pl.multiple_of(t * 256 + n * 16, 16), 16)
            pre[rows, :] = rms_rows(pre[rows, :].astype(F32), gain_p[...]).astype(BF16)
            return carry

        lax.fori_loop(0, 16, tile, 0)

    for t in range(4):
        norm_prefix(t)
        gather_step(0, t + 1)
    wo[0] = perturbed(co, do)
    sqkv[0, :, :HD] = sq[...]
    sqkv[0, :, HD:2 * HD] = sk[...]
    sqkv[0, :, 2 * HD:] = sv[...]
    so[0] = so_in[...]
    gather_end(0)

    def latent_slice(u, i):
        columns = pl.ds(pl.multiple_of(blk_from(i) * 512, 512), 512)
        return gat[u, :, :, :, columns].reshape(256, 512)

    def natural(values, width):
        cut = values.reshape(8, 2, 2, 8, width)
        swapped = jnp.concatenate(
            [cut[:, :, yy][:, :, None] for yy in range(2)], axis=2
        )
        order = jnp.stack([cut[:, cc, yy] for yy in range(2) for cc in range(2)], axis=1)
        del swapped
        return order.reshape(256, width)

    def query_part(i, carry):
        @pl.when(i > 0)
        def _():
            arrived(wq.at[i], S_WQ + i)

        part_q = dot(latent_slice(0, i), wq[i])

        @pl.when(i == 0)
        def _():
            qacc[:, :HD] = part_q

        @pl.when(i > 0)
        def _():
            qacc[:, :HD] = qacc[:, :HD] + part_q

        return carry

    lax.fori_loop(0, 8, query_part, 0)
    qn[0] = natural(qacc[:, :HD], HD).astype(BF16)
    for i in range(1, 8):
        send(qn.at[0], qn.at[i], S_Q + i, blk_to(i))
    for i in range(1, 8):
        send(wo.at[0], wo.at[i], S_WO + i, blk_to(i))

    def keyval_part(i, carry):
        @pl.when(i > 0)
        def _():
            arrived(wkv.at[i], S_WKV + i)

        columns = pl.ds(pl.multiple_of(blk_from(i) * 512, 512), 512)
        for t in range(5):
            rows = pl.ds(t * 256, 256)
            if t < 4:
                piece = dot(pre[rows, columns], wkv[i])
            else:
                piece = dot(latent_slice(0, i), wkv[i])

            @pl.when(i == 0)
            def _():
                acc[rows, :] = piece

            @pl.when(i > 0)
            def _():
                acc[rows, :] = acc[rows, :] + piece

        return carry

    lax.fori_loop(0, 8, keyval_part, 0)
    for t in range(5):
        rows = pl.ds(t * 256, 256)
        values = acc[rows, :]
        if t == 4:
            values = natural(values, 2 * HD)
        kn[rows, :] = values[:, :HD].astype(BF16)
        vt[:, rows] = values[:, HD:].T.astype(BF16)

    def attend(i, carry):
        @pl.when(i > 0)
        def _():
            arrived(qn.at[i], S_Q + i)
            arrived(lim.at[i], S_LIM + i)

        source = blk_from(i)
        queries = qn[i]
        seen = lim[i][0:1, :]
        high = jnp.full((8, 256), CLIP, F32)
        for t in range(5):
            s = dot(kn[pl.ds(t * 256, 256), :], queries, 1, 1) * SCALE
            ids = lax.broadcasted_iota(jnp.int32, (256, 256), 0)
            if t < 4:
                allowed = ids + (b * 1024 + t * 256) < seen
            else:
                allowed = ids + b * 256 <= lax.broadcasted_iota(jnp.int32, (256, 256), 1) + source * 256
            s = jnp.where(allowed, s, LOW)
            scores[pl.ds(t * 256, 256), :] = s
            high = jnp.maximum(high, jnp.max(s.reshape(32, 8, 256), axis=0))
        top = jnp.max(high, axis=0, keepdims=True)
        total = jnp.zeros((8, 256), F32)
        weighted = jnp.zeros((HD, 256), F32)
        for t in range(5):
            e = jnp.exp(scores[pl.ds(t * 256, 256), :] - top)
            total = total + jnp.sum(e.reshape(32, 8, 256), axis=0)
            weighted = weighted + dot(vt[:, pl.ds(t * 256, 256)], e.astype(BF16))
        total = jnp.sum(total, axis=0, keepdims=True)
        otx[i] = weighted.astype(BF16)
        first = lax.broadcasted_iota(jnp.int32, (8, 256), 0) == 0
        sttx[i] = jnp.where(first, top, total)

        @pl.when(i > 0)
        def _():
            back = {"blk": source, "grp": g}
            remote(otx.at[i], orx.at[i], S_O + i, back).start()
            remote(sttx.at[i], strx.at[i], S_ST + i, back).start()

        return carry

    lax.fori_loop(0, 8, attend, 0)
    for i in range(1, 8):
        back = {"blk": blk_from(i), "grp": g}
        sent.append(remote(otx.at[i], orx.at[i], S_O + i, back))
        sent.append(remote(sttx.at[i], strx.at[i], S_ST + i, back))
    for i in range(1, 8):
        send(sqkv.at[0], sqkv.at[i], S_SQKV + i, blk_to(i))

    orx[0] = otx[0]
    strx[0] = sttx[0]
    for i in range(1, 8):
        arrived(orx.at[i], S_O + i)
        arrived(strx.at[i], S_ST + i)
    tops = [strx[i][0:1, :] for i in range(8)]
    top = functools.reduce(jnp.maximum, tops)
    total = jnp.zeros((1, 256), F32)
    weighted = jnp.zeros((HD, 256), F32)
    for i in range(8):
        factor = jnp.exp(tops[i] - top)
        total = total + factor * strx[i][1:2, :]
        weighted = weighted + orx[i].astype(F32) * factor
    mixed[0] = (weighted / total).T.astype(BF16)

    def project_and_sum(u, weight, place):
        def columns_of(i, carry):
            @pl.when(i > 0)
            def _():
                arrived(weight.at[i], place + i)

            columns = pl.ds(pl.multiple_of(blk_from(i) * 512, 512), 512)
            y = dot(mixed[u], weight[i]).reshape(8, 2, 2, 8, 512)
            for cc in range(2):
                part[u, cc, :, :, columns] = y[:, :, cc].reshape(8, 16, 512).astype(BF16)
            return carry

        lax.fori_loop(0, 8, columns_of, 0)
        send(part.at[u, 1 - c], sib.at[u], S_RSC + u, sibling)
        arrived(sib.at[u], S_RSC + u)

        def chip_sum(zz, h):
            columns = pl.ds(h * HALF, HALF)
            return part[u, c, zz, :, columns].astype(F32) + sib[u, zz, :, columns].astype(F32)

        for k in (4, 3, 2, 1):
            for way, h in ((0, 0), (1, 1), (0, 1), (1, 0)):
                start = 4 if way == h else 3
                if k > start:
                    continue
                zz = (z + k) % 8 if way == 0 else (z + 8 - k) % 8
                value = chip_sum(zz, h)
                at = S_RSZ + ((u * 2 + way) * 2 + h) * 5
                if k < start:
                    arrived(rrx.at[u, way, h, k], at + k + 1)
                    value = value + rrx[u, way, h, k].astype(F32)
                rtx[u, way, h, k - 1] = value.astype(BF16)
                send(rtx.at[u, way, h, k - 1], rrx.at[u, way, h, k - 1], at + k, vertical[way])
        halves = []
        for h in range(2):
            value = chip_sum(z, h)
            for way in range(2):
                arrived(rrx.at[u, way, h, 0], S_RSZ + ((u * 2 + way) * 2 + h) * 5 + 1)
                value = value + rrx[u, way, h, 0].astype(F32)
            halves.append(value)
        both = jnp.concatenate(halves, axis=1)
        mine = jnp.where(yh == 0, both[:8], both[8:])
        ytx[u] = pack_rows(jnp.where(yh == 0, both[8:], both[:8])).astype(BF16)
        send(ytx.at[u], yrx.at[u], S_RSY + u, across)
        arrived(yrx.at[u], S_RSY + u)
        return mine + unpack_rows(yrx[u].astype(F32))

    carried[...] = latent[...].astype(F32) + project_and_sum(0, wo, S_WO)

    rows_c = rms_rows(carried[...], gain_s[...])
    pk[1] = pack_rows(rows_c).astype(BF16)
    gather_begin(1)
    gather_pair(1, rows_c)
    for k in range(1, 5):
        gather_step(1, k)
    gather_end(1)

    def self_part(i, carry):
        @pl.when(i > 0)
        def _():
            arrived(sqkv.at[i], S_SQKV + i)

        piece = dot(latent_slice(1, i), sqkv[i])

        @pl.when(i == 0)
        def _():
            qacc[...] = piece

        @pl.when(i > 0)
        def _():
            qacc[...] = qacc[...] + piece

        return carry

    lax.fori_loop(0, 8, self_part, 0)
    qkv = natural(qacc[...], 3 * HD)
    queries = qkv[:, :HD].astype(BF16)
    k2[0] = qkv[:, HD:2 * HD].astype(BF16)
    v2[0] = qkv[:, 2 * HD:].T.astype(BF16)

    def later(i):
        there = {"blk": jnp.minimum(b + i, 7), "grp": g}
        return (
            remote(k2.at[0], k2.at[i], S_K2 + i, there),
            remote(v2.at[0], v2.at[i], S_V2 + i, there),
        )

    for i in range(1, 8):
        @pl.when(b + i < 8)
        def _():
            for copy in later(i):
                copy.start()
    for i in range(1, 8):
        send(so.at[0], so.at[i], S_SO + i, blk_to(i))

    def absorb(s, values, top, total, weighted):
        new = jnp.maximum(top, jnp.max(s, axis=0, keepdims=True))
        e = jnp.exp(s - new)
        factor = jnp.exp(top - new)
        total = total * factor + jnp.sum(e, axis=0, keepdims=True)
        return new, total, weighted * factor + dot(values, e.astype(BF16))

    s = dot(k2[0], queries, 1, 1) * SCALE
    s = jnp.where(
        lax.broadcasted_iota(jnp.int32, (256, 256), 0) <= lax.broadcasted_iota(jnp.int32, (256, 256), 1),
        s, LOW,
    )
    state = absorb(
        s, v2[0], jnp.full((1, 256), CLIP, F32), jnp.zeros((1, 256), F32), jnp.zeros((HD, 256), F32)
    )

    def self_block(i, state):
        arrived(k2.at[i], S_K2 + i)
        arrived(v2.at[i], S_V2 + i)
        return absorb(dot(k2[i], queries, 1, 1) * SCALE, v2[i], *state)

    top, total, weighted = lax.fori_loop(1, b + 1, self_block, state)
    mixed[1] = (weighted / total).T.astype(BF16)

    out[...] = carried[...] + project_and_sum(1, so, S_SO)

    for i in range(1, 8):
        @pl.when(b + i < 8)
        def _():
            for copy in later(i):
                copy.wait_send()
    for copy in sent:
        copy.wait_send()


def shards(*arguments):
    prefix, latent, limits, gain_p, gain_l, gain_s, *weights = arguments
    vmem = pl.BlockSpec(memory_space=pltpu.VMEM)
    sem = pltpu.SemaphoreType.DMA
    scratch = [
        ((1024, D), BF16),
        ((8, 512, HD), BF16),
        ((8, 512, 2 * HD), BF16),
        ((8, HD, 512), BF16),
        ((8, 512, 3 * HD), BF16),
        ((8, HD, 512), BF16),
        ((8, 8, 256), jnp.int32),
        ((8, 256, HD), BF16),
        ((1280, HD), BF16),
        ((HD, 1280), BF16),
        ((1280, 2 * HD), F32),
        ((256, 3 * HD), F32),
        ((1280, 256), F32),
        ((8, HD, 256), BF16),
        ((8, HD, 256), BF16),
        ((8, 8, 256), F32),
        ((8, 8, 256), F32),
        ((2, 256, HD), BF16),
        ((8, 256, HD), BF16),
        ((8, HD, 256), BF16),
        ((HD, 256), F32),
        ((2, 16, HALF), BF16),
        ((2, 16, HALF), BF16),
        ((2, 8, 2, 16, D), BF16),
        ((2, 2, 8, 16, D), BF16),
        ((2, 8, 16, D), BF16),
        ((2, 2, 2, 4, 16, HALF), BF16),
        ((2, 2, 2, 4, 16, HALF), BF16),
        ((2, 16, HALF), BF16),
        ((2, 16, HALF), BF16),
        ((8, D), F32),
    ]
    return pl.pallas_call(
        layer_kernel,
        out_shape=jax.ShapeDtypeStruct((8, D), F32),
        in_specs=[pl.BlockSpec(memory_space=pl.ANY)] + [vmem] * 17,
        out_specs=vmem,
        scratch_shapes=[pltpu.VMEM(shape, dtype) for shape, dtype in scratch]
        + [sem((N_SEM,)), sem((N_SEM,)), sem((4,))],
        compiler_params=pltpu.CompilerParams(
            collective_id=0, has_side_effects=True, vmem_limit_bytes=56 * 1024 * 1024
        ),
        name="layer",
    )(
        prefix, latent, limits.reshape(1, -1),
        gain_p.reshape(1, -1), gain_l.reshape(1, -1), gain_s.reshape(1, -1), *weights,
    )


def solution(mesh):
    return jax.shard_map(
        shards,
        mesh=mesh,
        in_specs=(
            P("blk", None), P(("blk", "grp"), None), P("blk"), P(), P(), P(),
            P("blk", "grp"), P("blk", "grp"), P("blk", "grp"), P("grp", "blk"),
            P("blk", "grp"), P("blk", "grp"), P("blk", "grp"), P("grp", "blk"),
            P("blk", "grp"), P("blk", "grp"), P("blk", "grp"), P("grp", "blk"),
        ),
        out_specs=P(("blk", "grp"), None),
        check_vma=False,
    )
```

time: 960 us -> 201 us (0.21)
  waiting for transfers between devices: 865 us -> 0 us
  Pallas kernels: 0 us -> 199 us
  matrix products: 48.6 us -> 0 us
  other arithmetic: 23.9 us -> 0 us
  between operations: 14.1 us -> 0.01 us
    all_gather x10 -> x0, waiting for transfers between devices: 350 us -> none  [the longest x1 73 us: shards(): latent_all = lax.all_gather(latent, 'grp', axis=0, tiled=True)]
    psum x1 -> x0, waiting for transfers between devices: 271 us -> none  [shards(): lax.psum(jnp.dot(mixed_cross, w_out, preferred_element_type=jnp.float32),...]
    pallas_call x0 -> x1, Pallas kernels: none -> 199 us  [shards(): pl.pallas_call(layer_kernel, out_shape=jax.ShapeDtypeStruct((8, D), F32),...]
    ppermute x7 -> x0, waiting for transfers between devices: 123 us -> none  [passed_along(): return lax.ppermute(block, axis, route)]
    reduce_scatter x1 -> x0, waiting for transfers between devices: 118 us -> none  [shards(): lax.psum_scatter(jnp.dot(mixed_self, s_out, preferred_element_type=jnp.fl...]
    dot_general x40 -> x0, matrix products: 48.6 us -> none  [the longest x17 14.1 us: absorb(): jnp.einsum('qhk,khd->qhd', exponent, value_part.astype(jnp.float32), prec...]
    reduce_sum x8 -> x0, other arithmetic: 15.4 us -> none  [the longest x3 12 us: rms_scale(): jnp.mean(values * values, axis=-1, keepdims=True) + epsilon]
  transfers between devices with their start and end apart: 19 -> 0, of which waited for: 17 -> 0; matrix products, arithmetic and copies ran while one was open for 7% -> 0% of each run, Pallas kernels for 0% -> 0%
where the time goes in v1:
time: 201 us
  Pallas kernels  199 us (99%)
    pallas_call x1, Pallas kernels, shards(): pl.pallas_call(layer_kernel, out_shape=jax.ShapeDtypeStruct((8, D), F32),...  199 us

profile of v1, /device:TPU:40, one launch (start us, length us, event | category | flops | bytes accessed | tf_op | source)
XLA Modules:
  0.0 200.6 jit_solution(868151578954060877)
XLA Ops:
  0.0 199.0 %layer.1 = f32[8,4096]{1,0:T(8,128)} custom-call(bf16[1024,4096]{1,0:T(8,128)(2,1)} %prefix.1, bf16[8,4096]{1,0:T(8,128)(2,1)} %latent.1, s32[1,256]{1,0:T(1,128)} %bitcast.7, f32[1,4096]{1,0:T(1,128)} %bitcast.4, f32[1,4096]{1,0:T(1,128)} %bitcast.5, f32[1,4096]{1,0:T(1,128)} %bitcast.6, bf16[512,128]{1,0:T(8,128)(2,1)} %cq.1, bf16[512,128]{1,0:T(8,128)(2,1)} %ck.1, ...), custom_call_target="tpu_custom_call" | custom-call | tf_op jit(solution)/shard_map/layer/pallas_call | solution.py:500
  199.0 1.6 copy.20

commit v2 on v1

--- a/solution.py
+++ b/solution.py
@@ -28,11 +28,11 @@
     return first
 
 
-S_WQ = _places(8)
-S_WKV = _places(8)
-S_WO = _places(8)
-S_SQKV = _places(8)
-S_SO = _places(8)
+S_WX = _places(10)
+S_WY = _places(10)
+S_WO = _places(10)
+S_SQKV = _places(10)
+S_SO = _places(10)
 S_LIM = _places(8)
 S_Q = _places(8)
 S_O = _places(8)
@@ -42,7 +42,7 @@
 S_AGY = _places(2)
 S_AGZ = _places(2 * 2 * 5)
 S_AGC = _places(2 * 8)
-S_RSC = _places(2)
+S_RSC = _places(4)
 S_RSZ = _places(2 * 2 * 2 * 5)
 S_RSY = _places(2)
 
@@ -68,9 +68,9 @@
     prefix, latent, limits, gain_p, gain_l, gain_s,
     cq, ck, cv, co, dq, dk, dv, do, sq, sk, sv, so_in,
     out,
-    pre, wq, wkv, wo, sqkv, so, lim, qn, kn, vt, acc, qacc, scores,
-    otx, orx, sttx, strx, mixed, k2, v2, o2,
-    pk, pkr, gat, part, sib, rtx, rrx, ytx, yrx, carried,
+    pre, wqkv, wo, sqkv, so, lim, qn, kn, vt, acc, qacc, scores,
+    otx, orx, sttx, strx, mixed, k2, v2,
+    pk, pkr, gat, part, sib, rtx, rrx, ytx, yrx, ztx, zrx,
     ss, rs, ls,
 ):
     b = lax.axis_index("blk")
@@ -125,23 +125,81 @@
     def perturbed(weight, delta):
         return (weight[...].astype(F32) + delta[...].astype(F32)).astype(BF16)
 
-    rows_l = rms_rows(latent[...].astype(F32), gain_l[...])
-    pk[0] = pack_rows(rows_l).astype(BF16)
+    rows_l = latent[...].astype(F32)
+    pk[...] = pack_rows(rows_l).astype(BF16)
     lim[0] = jnp.broadcast_to(limits[...], (8, 256))
-    wq[0] = perturbed(cq, dq)
-    wkv[0, :, :HD] = perturbed(ck, dk)
-    wkv[0, :, HD:] = perturbed(cv, dv)
+    wqkv[0, :, :HD] = perturbed(cq, dq)
+    wqkv[0, :, HD:2 * HD] = perturbed(ck, dk)
+    wqkv[0, :, 2 * HD:] = perturbed(cv, dv)
     pl.semaphore_wait(barrier, 11)
 
-    def gather_begin(u):
-        send(pk.at[u], pkr.at[u], S_AGY + u, across)
-
-    def gather_pair(u, rows):
-        arrived(pkr.at[u], S_AGY + u)
-        other = unpack_rows(pkr[u].astype(F32))
-        low = jnp.where(yh == 0, rows, other)
-        high = jnp.where(yh == 0, other, rows)
-        gat[u, z, c] = jnp.concatenate([low, high], axis=0).astype(BF16)
+    right, left, beside = blk_to(1), blk_to(3), blk_to(4)
+
+    def spread(buf, start, rows, place, y_first, stage):
+        def cut(i, piece=None):
+            if piece is None:
+                return buf.at[i, pl.ds(start, rows)]
+            return buf.at[i, pl.ds(start + piece * (rows // 2), rows // 2)]
+
+        if stage == 0:
+            send(cut(0), cut(4), place + 4, beside)
+            send(cut(0), cut(1), place + 1, right)
+            send(cut(0), cut(3), place + 3, left)
+        elif y_first and stage == 1:
+            arrived(cut(4), place + 4)
+            send(cut(4), cut(5), place + 5, right)
+            send(cut(4), cut(7), place + 7, left)
+        elif y_first and stage == 2:
+            arrived(cut(1), place + 1)
+            send(cut(1, 0), cut(2, 0), place + 2, right)
+            arrived(cut(3), place + 3)
+            send(cut(3, 1), cut(2, 1), place + 8, left)
+        elif y_first and stage == 3:
+            arrived(cut(5), place + 5)
+            send(cut(5, 0), cut(6, 0), place + 6, right)
+            arrived(cut(7), place + 7)
+            send(cut(7, 1), cut(6, 1), place + 9, left)
+        elif y_first:
+            arrived(cut(2, 0), place + 2)
+            arrived(cut(2, 1), place + 8)
+            arrived(cut(6, 0), place + 6)
+            arrived(cut(6, 1), place + 9)
+        elif stage == 1:
+            arrived(cut(1), place + 1)
+            send(cut(1, 0), cut(2, 0), place + 2, right)
+            send(cut(1), cut(5), place + 5, beside)
+            arrived(cut(3), place + 3)
+            send(cut(3, 1), cut(2, 1), place + 8, left)
+            send(cut(3), cut(7), place + 7, beside)
+        elif stage == 2:
+            arrived(cut(2, 0), place + 2)
+            arrived(cut(2, 1), place + 8)
+            send(cut(2), cut(6), place + 6, beside)
+        elif stage == 3:
+            arrived(cut(4), place + 4)
+            arrived(cut(5), place + 5)
+            arrived(cut(7), place + 7)
+        else:
+            arrived(cut(6), place + 6)
+
+    def spread_cross(stage):
+        spread(wqkv, 0, 256, S_WX, False, stage)
+        spread(wqkv, 256, 256, S_WY, True, stage)
+
+    def spread_self(stage):
+        spread(sqkv, 0, 512, S_SQKV, True, stage)
+
+    def spread_wo(stage):
+        spread(wo, 0, HD, S_WO, True, stage)
+
+    def spread_so(stage):
+        spread(so, 0, HD, S_SO, True, stage)
+
+    def own_and_other(own, other):
+        return jnp.concatenate([jnp.where(yh == 0, own, other), jnp.where(yh == 0, other, own)], axis=0)
+
+    def gather_begin(u, rows, gain):
+        gat[u, z, c] = rms_rows(rows, gain).astype(BF16)
         own = gat.at[u, z, c]
         for way in range(2):
             send(own, own, S_AGZ + (u * 2 + way) * 5 + 1, vertical[way])
@@ -169,14 +227,10 @@
         for k in range(8):
             arrived(gat.at[u, (z + 8 - k) % 8, 1 - c], S_AGC + u * 8 + k)
 
-    gather_begin(0)
+    send(pk, pkr, S_AGY, across)
+    spread_cross(0)
     for i in range(1, 8):
         send(lim.at[0], lim.at[i], S_LIM + i, blk_to(i))
-    for i in range(1, 8):
-        send(wq.at[0], wq.at[i], S_WQ + i, blk_to(i))
-    for i in range(1, 8):
-        send(wkv.at[0], wkv.at[i], S_WKV + i, blk_to(i))
-    gather_pair(0, rows_l)
 
     def norm_prefix(t):
         loads[t].wait()
@@ -188,15 +242,50 @@
 
         lax.fori_loop(0, 16, tile, 0)
 
-    for t in range(4):
-        norm_prefix(t)
-        gather_step(0, t + 1)
+    def prefix_part(i):
+        columns = pl.ds(pl.multiple_of(blk_from(i) * 512, 512), 512)
+        for t in range(4):
+            rows = pl.ds(t * 256, 256)
+            piece = dot(pre[rows, columns], wqkv[i, :, HD:])
+
+            @pl.when(i == 0)
+            def _():
+                acc[rows, :] = piece
+
+            @pl.when(i > 0)
+            def _():
+                acc[rows, :] = acc[rows, :] + piece
+
+    def prefix_parts(count, slot_of):
+        def one(n, carry):
+            prefix_part(slot_of(n))
+            return carry
+
+        lax.fori_loop(0, count, one, 0)
+
+    norm_prefix(0)
+    arrived(pkr, S_AGY)
+    latent_pair = own_and_other(rows_l, unpack_rows(pkr[...].astype(F32)))
+    gather_begin(0, latent_pair, gain_l[...])
+    spread_cross(1)
+    norm_prefix(1)
+    gather_step(0, 1)
+    spread_cross(2)
+    norm_prefix(2)
+    gather_step(0, 2)
+    spread_cross(3)
+    norm_prefix(3)
+    gather_step(0, 3)
     wo[0] = perturbed(co, do)
     sqkv[0, :, :HD] = sq[...]
     sqkv[0, :, HD:2 * HD] = sk[...]
     sqkv[0, :, 2 * HD:] = sv[...]
     so[0] = so_in[...]
+    gather_step(0, 4)
+    prefix_parts(4, lambda n: n + n // 2)
+    prefix_parts(2, lambda n: 5 + 2 * n)
     gather_end(0)
+    spread_cross(4)
 
     def latent_slice(u, i):
         columns = pl.ds(pl.multiple_of(blk_from(i) * 512, 512), 512)
@@ -204,68 +293,40 @@
 
     def natural(values, width):
         cut = values.reshape(8, 2, 2, 8, width)
-        swapped = jnp.concatenate(
-            [cut[:, :, yy][:, :, None] for yy in range(2)], axis=2
-        )
         order = jnp.stack([cut[:, cc, yy] for yy in range(2) for cc in range(2)], axis=1)
-        del swapped
         return order.reshape(256, width)
 
-    def query_part(i, carry):
-        @pl.when(i > 0)
-        def _():
-            arrived(wq.at[i], S_WQ + i)
-
-        part_q = dot(latent_slice(0, i), wq[i])
-
-        @pl.when(i == 0)
-        def _():
-            qacc[:, :HD] = part_q
-
-        @pl.when(i > 0)
-        def _():
-            qacc[:, :HD] = qacc[:, :HD] + part_q
-
-        return carry
-
-    lax.fori_loop(0, 8, query_part, 0)
-    qn[0] = natural(qacc[:, :HD], HD).astype(BF16)
-    for i in range(1, 8):
-        send(qn.at[0], qn.at[i], S_Q + i, blk_to(i))
-    for i in range(1, 8):
-        send(wo.at[0], wo.at[i], S_WO + i, blk_to(i))
-
-    def keyval_part(i, carry):
-        @pl.when(i > 0)
-        def _():
-            arrived(wkv.at[i], S_WKV + i)
-
-        columns = pl.ds(pl.multiple_of(blk_from(i) * 512, 512), 512)
-        for t in range(5):
-            rows = pl.ds(t * 256, 256)
-            if t < 4:
-                piece = dot(pre[rows, columns], wkv[i])
-            else:
-                piece = dot(latent_slice(0, i), wkv[i])
+    def row_projections(u, weights):
+        def one(i, carry):
+            piece = dot(latent_slice(u, i), weights[i])
 
             @pl.when(i == 0)
             def _():
-                acc[rows, :] = piece
+                qacc[...] = piece
 
             @pl.when(i > 0)
             def _():
-                acc[rows, :] = acc[rows, :] + piece
-
-        return carry
-
-    lax.fori_loop(0, 8, keyval_part, 0)
-    for t in range(5):
+                qacc[...] = qacc[...] + piece
+
+            return carry
+
+        lax.fori_loop(0, 8, one, 0)
+        return natural(qacc[...], 3 * HD)
+
+    latent_qkv = row_projections(0, wqkv)
+    qn[0] = latent_qkv[:, :HD].astype(BF16)
+    for i in range(1, 8):
+        send(qn.at[0], qn.at[i], S_Q + i, blk_to(i))
+    spread_wo(0)
+    kn[pl.ds(1024, 256), :] = latent_qkv[:, HD:2 * HD].astype(BF16)
+    vt[:, pl.ds(1024, 256)] = latent_qkv[:, 2 * HD:].T.astype(BF16)
+    prefix_parts(2, lambda n: 2 + 4 * n)
+    for t in range(4):
         rows = pl.ds(t * 256, 256)
         values = acc[rows, :]
-        if t == 4:
-            values = natural(values, 2 * HD)
         kn[rows, :] = values[:, :HD].astype(BF16)
         vt[:, rows] = values[:, HD:].T.astype(BF16)
+    spread_wo(1)
 
     def attend(i, carry):
         @pl.when(i > 0)
@@ -307,13 +368,15 @@
 
         return carry
 
-    lax.fori_loop(0, 8, attend, 0)
+    lax.fori_loop(0, 4, attend, 0)
+    spread_wo(2)
+    lax.fori_loop(4, 8, attend, 0)
+    spread_wo(3)
     for i in range(1, 8):
         back = {"blk": blk_from(i), "grp": g}
         sent.append(remote(otx.at[i], orx.at[i], S_O + i, back))
         sent.append(remote(sttx.at[i], strx.at[i], S_ST + i, back))
-    for i in range(1, 8):
-        send(sqkv.at[0], sqkv.at[i], S_SQKV + i, blk_to(i))
+    spread_self(0)
 
     orx[0] = otx[0]
     strx[0] = sttx[0]
@@ -329,30 +392,36 @@
         total = total + factor * strx[i][1:2, :]
         weighted = weighted + orx[i].astype(F32) * factor
     mixed[0] = (weighted / total).T.astype(BF16)
-
-    def project_and_sum(u, weight, place):
-        def columns_of(i, carry):
-            @pl.when(i > 0)
-            def _():
-                arrived(weight.at[i], place + i)
-
-            columns = pl.ds(pl.multiple_of(blk_from(i) * 512, 512), 512)
-            y = dot(mixed[u], weight[i]).reshape(8, 2, 2, 8, 512)
-            for cc in range(2):
-                part[u, cc, :, :, columns] = y[:, :, cc].reshape(8, 16, 512).astype(BF16)
-            return carry
-
-        lax.fori_loop(0, 8, columns_of, 0)
-        send(part.at[u, 1 - c], sib.at[u], S_RSC + u, sibling)
-        arrived(sib.at[u], S_RSC + u)
+    spread_wo(4)
+    spread_self(1)
+
+    def half_columns(h):
+        return pl.ds(pl.multiple_of(((h + yl) % 2) * HALF, HALF), HALF)
+
+    def project_and_sum(u, weight, between):
+        for h in range(2):
+            def columns_of(i, carry):
+                columns = pl.ds(pl.multiple_of(blk_from(i) * 512, 512), 512)
+                y = dot(mixed[u], weight[i]).reshape(8, 2, 2, 8, 512)
+                for cc in range(2):
+                    part[u, cc, :, :, columns] = y[:, :, cc].reshape(8, 16, 512).astype(BF16)
+                return carry
+
+            lax.fori_loop(4 * h, 4 * h + 4, columns_of, 0)
+            send(
+                part.at[u, 1 - c, :, :, half_columns(h)], sib.at[u, :, :, half_columns(h)],
+                S_RSC + 2 * u + h, sibling,
+            )
 
         def chip_sum(zz, h):
-            columns = pl.ds(h * HALF, HALF)
+            columns = half_columns(h)
             return part[u, c, zz, :, columns].astype(F32) + sib[u, zz, :, columns].astype(F32)
 
         for k in (4, 3, 2, 1):
-            for way, h in ((0, 0), (1, 1), (0, 1), (1, 0)):
+            for h, way in ((0, 0), (0, 1), (1, 1), (1, 0)):
                 start = 4 if way == h else 3
+                if k == 4 and way == h:
+                    arrived(sib.at[u, :, :, half_columns(h)], S_RSC + 2 * u + h)
                 if k > start:
                     continue
                 zz = (z + k) % 8 if way == 0 else (z + 8 - k) % 8
@@ -363,6 +432,7 @@
                     value = value + rrx[u, way, h, k].astype(F32)
                 rtx[u, way, h, k - 1] = value.astype(BF16)
                 send(rtx.at[u, way, h, k - 1], rrx.at[u, way, h, k - 1], at + k, vertical[way])
+            between(k)
         halves = []
         for h in range(2):
             value = chip_sum(z, h)
@@ -370,42 +440,38 @@
                 arrived(rrx.at[u, way, h, 0], S_RSZ + ((u * 2 + way) * 2 + h) * 5 + 1)
                 value = value + rrx[u, way, h, 0].astype(F32)
             halves.append(value)
-        both = jnp.concatenate(halves, axis=1)
-        mine = jnp.where(yh == 0, both[:8], both[8:])
-        ytx[u] = pack_rows(jnp.where(yh == 0, both[8:], both[:8])).astype(BF16)
-        send(ytx.at[u], yrx.at[u], S_RSY + u, across)
-        arrived(yrx.at[u], S_RSY + u)
-        return mine + unpack_rows(yrx[u].astype(F32))
-
-    carried[...] = latent[...].astype(F32) + project_and_sum(0, wo, S_WO)
-
-    rows_c = rms_rows(carried[...], gain_s[...])
-    pk[1] = pack_rows(rows_c).astype(BF16)
-    gather_begin(1)
-    gather_pair(1, rows_c)
+        return jnp.concatenate(
+            [jnp.where(yl == 0, halves[0], halves[1]), jnp.where(yl == 0, halves[1], halves[0])], axis=1
+        )
+
+    def between_cross(k):
+        if k == 4:
+            spread_self(2)
+        if k == 3:
+            spread_so(0)
+        if k == 2:
+            spread_self(3)
+        if k == 1:
+            spread_so(1)
+
+    both = project_and_sum(0, wo, between_cross)
+    ztx[...] = both.astype(BF16)
+    send(ztx, zrx, S_RSY, across)
+    arrived(zrx, S_RSY)
+    carried = latent_pair + both + zrx[...].astype(F32)
+    own_carried = jnp.where(yh == 0, carried[:8], carried[8:])
+
+    gather_begin(1, carried, gain_s[...])
     for k in range(1, 5):
         gather_step(1, k)
+        if k == 2:
+            spread_so(2)
+        if k == 3:
+            spread_so(3)
     gather_end(1)
-
-    def self_part(i, carry):
-        @pl.when(i > 0)
-        def _():
-            arrived(sqkv.at[i], S_SQKV + i)
-
-        piece = dot(latent_slice(1, i), sqkv[i])
-
-        @pl.when(i == 0)
-        def _():
-            qacc[...] = piece
-
-        @pl.when(i > 0)
-        def _():
-            qacc[...] = qacc[...] + piece
-
-        return carry
-
-    lax.fori_loop(0, 8, self_part, 0)
-    qkv = natural(qacc[...], 3 * HD)
+    spread_self(4)
+
+    qkv = row_projections(1, sqkv)
     queries = qkv[:, :HD].astype(BF16)
     k2[0] = qkv[:, HD:2 * HD].astype(BF16)
     v2[0] = qkv[:, 2 * HD:].T.astype(BF16)
@@ -422,8 +488,6 @@
         def _():
             for copy in later(i):
                 copy.start()
-    for i in range(1, 8):
-        send(so.at[0], so.at[i], S_SO + i, blk_to(i))
 
     def absorb(s, values, top, total, weighted):
         new = jnp.maximum(top, jnp.max(s, axis=0, keepdims=True))
@@ -449,7 +513,12 @@
     top, total, weighted = lax.fori_loop(1, b + 1, self_block, state)
     mixed[1] = (weighted / total).T.astype(BF16)
 
-    out[...] = carried[...] + project_and_sum(1, so, S_SO)
+    spread_so(4)
+    both = project_and_sum(1, so, lambda k: None)
+    ytx[...] = pack_rows(jnp.where(yh == 0, both[8:], both[:8])).astype(BF16)
+    send(ytx, yrx, S_RSY + 1, across)
+    arrived(yrx, S_RSY + 1)
+    out[...] = own_carried + jnp.where(yh == 0, both[:8], both[8:]) + unpack_rows(yrx[...].astype(F32))
 
     for i in range(1, 8):
         @pl.when(b + i < 8)
@@ -466,8 +535,7 @@
     sem = pltpu.SemaphoreType.DMA
     scratch = [
         ((1024, D), BF16),
-        ((8, 512, HD), BF16),
-        ((8, 512, 2 * HD), BF16),
+        ((8, 512, 3 * HD), BF16),
         ((8, HD, 512), BF16),
         ((8, 512, 3 * HD), BF16),
         ((8, HD, 512), BF16),
@@ -475,7 +543,7 @@
         ((8, 256, HD), BF16),
         ((1280, HD), BF16),
         ((HD, 1280), BF16),
-        ((1280, 2 * HD), F32),
+        ((1024, 2 * HD), F32),
         ((256, 3 * HD), F32),
         ((1280, 256), F32),
         ((8, HD, 256), BF16),
@@ -485,17 +553,17 @@
         ((2, 256, HD), BF16),
         ((8, 256, HD), BF16),
         ((8, HD, 256), BF16),
-        ((HD, 256), F32),
-        ((2, 16, HALF), BF16),
-        ((2, 16, HALF), BF16),
+        ((16, HALF), BF16),
+        ((16, HALF), BF16),
         ((2, 8, 2, 16, D), BF16),
         ((2, 2, 8, 16, D), BF16),
         ((2, 8, 16, D), BF16),
         ((2, 2, 2, 4, 16, HALF), BF16),
         ((2, 2, 2, 4, 16, HALF), BF16),
-        ((2, 16, HALF), BF16),
-        ((2, 16, HALF), BF16),
-        ((8, D), F32),
+        ((16, HALF), BF16),
+        ((16, HALF), BF16),
+        ((16, D), BF16),
+        ((16, D), BF16),
     ]
     return pl.pallas_call(
         layer_kernel,

time: 201 us -> 164 us (0.82); the launches traced: 201 us -> 162 us
  Pallas kernels: 199 us -> 160 us
    pallas_call x1, Pallas kernels: 199 us -> 160 us  [shards(): pl.pallas_call(layer_kernel, out_shape=jax.ShapeDtypeStruct((8, D), F32),...]
where the time goes in v2:
time: 164 us; the launch traced here: 162 us
  Pallas kernels  160 us (98%)
    pallas_call x1, Pallas kernels, shards(): pl.pallas_call(layer_kernel, out_shape=jax.ShapeDtypeStruct((8, D), F32),...  160 us

profile of v2, /device:TPU:40, one launch (start us, length us, event | category | flops | bytes accessed | tf_op | source)
XLA Modules:
  0.0 161.5 jit_solution(16851185712973381522)
XLA Ops:
  0.0 159.9 %layer.1 = f32[8,4096]{1,0:T(8,128)} custom-call(bf16[1024,4096]{1,0:T(8,128)(2,1)} %prefix.1, bf16[8,4096]{1,0:T(8,128)(2,1)} %latent.1, s32[1,256]{1,0:T(1,128)} %bitcast.7, f32[1,4096]{1,0:T(1,128)} %bitcast.4, f32[1,4096]{1,0:T(1,128)} %bitcast.5, f32[1,4096]{1,0:T(1,128)} %bitcast.6, bf16[512,128]{1,0:T(8,128)(2,1)} %cq.1, bf16[512,128]{1,0:T(8,128)(2,1)} %ck.1, ...), custom_call_target="tpu_custom_call" | custom-call | tf_op jit(solution)/shard_map/layer/pallas_call | solution.py:568
  159.9 1.6 copy.20

commit v3 on v2

--- a/solution.py
+++ b/solution.py
@@ -28,8 +28,7 @@
     return first
 
 
-S_WX = _places(10)
-S_WY = _places(10)
+S_W = _places(4 * 10)
 S_WO = _places(10)
 S_SQKV = _places(10)
 S_SO = _places(10)
@@ -37,8 +36,7 @@
 S_Q = _places(8)
 S_O = _places(8)
 S_ST = _places(8)
-S_K2 = _places(8)
-S_V2 = _places(8)
+S_KV2 = _places(10)
 S_AGY = _places(2)
 S_AGZ = _places(2 * 2 * 5)
 S_AGC = _places(2 * 8)
@@ -68,8 +66,8 @@
     prefix, latent, limits, gain_p, gain_l, gain_s,
     cq, ck, cv, co, dq, dk, dv, do, sq, sk, sv, so_in,
     out,
-    pre, wqkv, wo, sqkv, so, lim, qn, kn, vt, acc, qacc, scores,
-    otx, orx, sttx, strx, mixed, k2, v2,
+    pre, wqkv, wo, sqkv, so, lim, qn, kn, vt, acc, scores,
+    otx, orx, sttx, strx, mixed, kv2, top2, total2, weighted2,
     pk, pkr, gat, part, sib, rtx, rrx, ytx, yrx, ztx, zrx,
     ss, rs, ls,
 ):
@@ -128,63 +126,61 @@
     rows_l = latent[...].astype(F32)
     pk[...] = pack_rows(rows_l).astype(BF16)
     lim[0] = jnp.broadcast_to(limits[...], (8, 256))
-    wqkv[0, :, :HD] = perturbed(cq, dq)
-    wqkv[0, :, HD:2 * HD] = perturbed(ck, dk)
-    wqkv[0, :, 2 * HD:] = perturbed(cv, dv)
+    wqkv[b, :, :HD] = perturbed(cq, dq)
+    wqkv[b, :, HD:2 * HD] = perturbed(ck, dk)
+    wqkv[b, :, 2 * HD:] = perturbed(cv, dv)
     pl.semaphore_wait(barrier, 11)
 
     right, left, beside = blk_to(1), blk_to(3), blk_to(4)
 
     def spread(buf, start, rows, place, y_first, stage):
-        def cut(i, piece=None):
+        def here(i, piece=None):
             if piece is None:
-                return buf.at[i, pl.ds(start, rows)]
-            return buf.at[i, pl.ds(start + piece * (rows // 2), rows // 2)]
+                return buf.at[blk_from(i), pl.ds(start, rows)]
+            return buf.at[blk_from(i), pl.ds(start + piece * (rows // 2), rows // 2)]
 
         if stage == 0:
-            send(cut(0), cut(4), place + 4, beside)
-            send(cut(0), cut(1), place + 1, right)
-            send(cut(0), cut(3), place + 3, left)
+            send(here(0), here(0), place + 4, beside)
+            send(here(0), here(0), place + 1, right)
+            send(here(0), here(0), place + 3, left)
         elif y_first and stage == 1:
-            arrived(cut(4), place + 4)
-            send(cut(4), cut(5), place + 5, right)
-            send(cut(4), cut(7), place + 7, left)
+            arrived(here(4), place + 4)
+            send(here(4), here(4), place + 5, right)
+            send(here(4), here(4), place + 7, left)
         elif y_first and stage == 2:
-            arrived(cut(1), place + 1)
-            send(cut(1, 0), cut(2, 0), place + 2, right)
-            arrived(cut(3), place + 3)
-            send(cut(3, 1), cut(2, 1), place + 8, left)
+            arrived(here(1), place + 1)
+            send(here(1, 0), here(1, 0), place + 2, right)
+            arrived(here(3), place + 3)
+            send(here(3, 1), here(3, 1), place + 8, left)
         elif y_first and stage == 3:
-            arrived(cut(5), place + 5)
-            send(cut(5, 0), cut(6, 0), place + 6, right)
-            arrived(cut(7), place + 7)
-            send(cut(7, 1), cut(6, 1), place + 9, left)
+            arrived(here(5), place + 5)
+            send(here(5, 0), here(5, 0), place + 6, right)
+            arrived(here(7), place + 7)
+            send(here(7, 1), here(7, 1), place + 9, left)
+        elif y_first and stage == 4:
+            arrived(here(2, 0), place + 2)
+            arrived(here(2, 1), place + 8)
         elif y_first:
-            arrived(cut(2, 0), place + 2)
-            arrived(cut(2, 1), place + 8)
-            arrived(cut(6, 0), place + 6)
-            arrived(cut(6, 1), place + 9)
+            arrived(here(6, 0), place + 6)
+            arrived(here(6, 1), place + 9)
         elif stage == 1:
-            arrived(cut(1), place + 1)
-            send(cut(1, 0), cut(2, 0), place + 2, right)
-            send(cut(1), cut(5), place + 5, beside)
-            arrived(cut(3), place + 3)
-            send(cut(3, 1), cut(2, 1), place + 8, left)
-            send(cut(3), cut(7), place + 7, beside)
+            arrived(here(1), place + 1)
+            send(here(1, 0), here(1, 0), place + 2, right)
+            send(here(1), here(1), place + 5, beside)
+            arrived(here(3), place + 3)
+            send(here(3, 1), here(3, 1), place + 8, left)
+            send(here(3), here(3), place + 7, beside)
         elif stage == 2:
-            arrived(cut(2, 0), place + 2)
-            arrived(cut(2, 1), place + 8)
-            send(cut(2), cut(6), place + 6, beside)
-        elif stage == 3:
-            arrived(cut(4), place + 4)
-            arrived(cut(5), place + 5)
-            arrived(cut(7), place + 7)
-        else:
-            arrived(cut(6), place + 6)
-
-    def spread_cross(stage):
-        spread(wqkv, 0, 256, S_WX, False, stage)
-        spread(wqkv, 256, 256, S_WY, True, stage)
+            arrived(here(2, 0), place + 2)
+            arrived(here(2, 1), place + 8)
+            send(here(2), here(2), place + 6, beside)
+        elif stage == 5:
+            for i in (4, 5, 7, 6):
+                arrived(here(i), place + i)
+
+    def spread_cross(stage, parts):
+        for n in parts:
+            spread(wqkv, n * 128, 128, S_W + 10 * n, n % 2 == 1, stage)
 
     def spread_self(stage):
         spread(sqkv, 0, 512, S_SQKV, True, stage)
@@ -228,107 +224,82 @@
             arrived(gat.at[u, (z + 8 - k) % 8, 1 - c], S_AGC + u * 8 + k)
 
     send(pk, pkr, S_AGY, across)
-    spread_cross(0)
+    spread_cross(0, (0, 1, 2, 3))
     for i in range(1, 8):
         send(lim.at[0], lim.at[i], S_LIM + i, blk_to(i))
 
     def norm_prefix(t):
-        loads[t].wait()
+        if t % 2 == 0:
+            loads[t // 2].wait()
 
         def tile(n, carry):
-            rows = pl.ds(pl.multiple_of(t * 256 + n * 16, 16), 16)
+            rows = pl.ds(pl.multiple_of(t * 128 + n * 16, 16), 16)
             pre[rows, :] = rms_rows(pre[rows, :].astype(F32), gain_p[...]).astype(BF16)
             return carry
 
-        lax.fori_loop(0, 16, tile, 0)
-
-    def prefix_part(i):
-        columns = pl.ds(pl.multiple_of(blk_from(i) * 512, 512), 512)
-        for t in range(4):
-            rows = pl.ds(t * 256, 256)
-            piece = dot(pre[rows, columns], wqkv[i, :, HD:])
-
-            @pl.when(i == 0)
-            def _():
-                acc[rows, :] = piece
-
-            @pl.when(i > 0)
-            def _():
-                acc[rows, :] = acc[rows, :] + piece
-
-    def prefix_parts(count, slot_of):
-        def one(n, carry):
-            prefix_part(slot_of(n))
-            return carry
-
-        lax.fori_loop(0, count, one, 0)
+        lax.fori_loop(0, 8, tile, 0)
+
+    def prefix_part(row, first):
+        columns = pl.ds(pl.multiple_of(row * HALF, HALF), HALF)
+        weights = wqkv[pl.ds(row * 4, 4), :, HD:].reshape(HALF, 2 * HD)
+        for t in range(2):
+            rows = pl.ds(t * 512, 512)
+            piece = dot(pre[rows, columns], weights)
+            acc[rows, :] = piece if first else acc[rows, :] + piece
+
+    def latent_rows(u):
+        return gat[u].reshape(256, D)
+
+    def natural(values, width):
+        cut = values.reshape(8, 2, 2, 8, width)
+        order = jnp.stack([cut[:, cc, yy] for yy in range(2) for cc in range(2)], axis=1)
+        return order.reshape(256, width)
 
     norm_prefix(0)
     arrived(pkr, S_AGY)
     latent_pair = own_and_other(rows_l, unpack_rows(pkr[...].astype(F32)))
     gather_begin(0, latent_pair, gain_l[...])
-    spread_cross(1)
     norm_prefix(1)
+    spread_cross(1, (0, 1))
+    norm_prefix(2)
     gather_step(0, 1)
-    spread_cross(2)
-    norm_prefix(2)
+    spread_cross(1, (2, 3))
+    norm_prefix(3)
+    spread_cross(2, (0, 1))
     gather_step(0, 2)
-    spread_cross(3)
-    norm_prefix(3)
+    norm_prefix(4)
+    spread_cross(2, (2, 3))
+    norm_prefix(5)
     gather_step(0, 3)
-    wo[0] = perturbed(co, do)
-    sqkv[0, :, :HD] = sq[...]
-    sqkv[0, :, HD:2 * HD] = sk[...]
-    sqkv[0, :, 2 * HD:] = sv[...]
-    so[0] = so_in[...]
+    spread_cross(3, (0, 1))
+    norm_prefix(6)
     gather_step(0, 4)
-    prefix_parts(4, lambda n: n + n // 2)
-    prefix_parts(2, lambda n: 5 + 2 * n)
+    spread_cross(3, (2, 3))
+    norm_prefix(7)
+    wo[b] = perturbed(co, do)
+    sqkv[b, :, :HD] = sq[...]
+    sqkv[b, :, HD:2 * HD] = sk[...]
+    sqkv[b, :, 2 * HD:] = sv[...]
+    so[b] = so_in[...]
     gather_end(0)
-    spread_cross(4)
-
-    def latent_slice(u, i):
-        columns = pl.ds(pl.multiple_of(blk_from(i) * 512, 512), 512)
-        return gat[u, :, :, :, columns].reshape(256, 512)
-
-    def natural(values, width):
-        cut = values.reshape(8, 2, 2, 8, width)
-        order = jnp.stack([cut[:, cc, yy] for yy in range(2) for cc in range(2)], axis=1)
-        return order.reshape(256, width)
-
-    def row_projections(u, weights):
-        def one(i, carry):
-            piece = dot(latent_slice(u, i), weights[i])
-
-            @pl.when(i == 0)
-            def _():
-                qacc[...] = piece
-
-            @pl.when(i > 0)
-            def _():
-                qacc[...] = qacc[...] + piece
-
-            return carry
-
-        lax.fori_loop(0, 8, one, 0)
-        return natural(qacc[...], 3 * HD)
-
-    latent_qkv = row_projections(0, wqkv)
-    qn[0] = latent_qkv[:, :HD].astype(BF16)
+    spread_cross(4, (0, 1, 2, 3))
+    prefix_part(yl, True)
+    spread_cross(5, (0, 1, 2, 3))
+    qn[0] = natural(dot(latent_rows(0), wqkv[:, :, :HD].reshape(D, HD)), HD).astype(BF16)
     for i in range(1, 8):
         send(qn.at[0], qn.at[i], S_Q + i, blk_to(i))
     spread_wo(0)
-    kn[pl.ds(1024, 256), :] = latent_qkv[:, HD:2 * HD].astype(BF16)
-    vt[:, pl.ds(1024, 256)] = latent_qkv[:, 2 * HD:].T.astype(BF16)
-    prefix_parts(2, lambda n: 2 + 4 * n)
-    for t in range(4):
+    prefix_part(1 - yl, False)
+    latent_kv = natural(dot(latent_rows(0), wqkv[:, :, HD:].reshape(D, 2 * HD)), 2 * HD)
+    for t in range(5):
         rows = pl.ds(t * 256, 256)
-        values = acc[rows, :]
+        values = acc[rows, :] if t < 4 else latent_kv
         kn[rows, :] = values[:, :HD].astype(BF16)
         vt[:, rows] = values[:, HD:].T.astype(BF16)
-    spread_wo(1)
-
-    def attend(i, carry):
+
+    def attend(n, carry):
+        i = (n + 1) % 8
+
         @pl.when(i > 0)
         def _():
             arrived(qn.at[i], S_Q + i)
@@ -368,16 +339,15 @@
 
         return carry
 
-    lax.fori_loop(0, 4, attend, 0)
+    lax.fori_loop(0, 3, attend, 0)
+    spread_wo(1)
     spread_wo(2)
-    lax.fori_loop(4, 8, attend, 0)
+    lax.fori_loop(3, 8, attend, 0)
     spread_wo(3)
     for i in range(1, 8):
         back = {"blk": blk_from(i), "grp": g}
         sent.append(remote(otx.at[i], orx.at[i], S_O + i, back))
         sent.append(remote(sttx.at[i], strx.at[i], S_ST + i, back))
-    spread_self(0)
-
     orx[0] = otx[0]
     strx[0] = sttx[0]
     for i in range(1, 8):
@@ -392,16 +362,17 @@
         total = total + factor * strx[i][1:2, :]
         weighted = weighted + orx[i].astype(F32) * factor
     mixed[0] = (weighted / total).T.astype(BF16)
+    spread_self(0)
     spread_wo(4)
-    spread_self(1)
+    spread_wo(5)
 
     def half_columns(h):
-        return pl.ds(pl.multiple_of(((h + yl) % 2) * HALF, HALF), HALF)
+        return pl.ds(h * HALF, HALF)
 
     def project_and_sum(u, weight, between):
         for h in range(2):
             def columns_of(i, carry):
-                columns = pl.ds(pl.multiple_of(blk_from(i) * 512, 512), 512)
+                columns = pl.ds(pl.multiple_of(i * 512, 512), 512)
                 y = dot(mixed[u], weight[i]).reshape(8, 2, 2, 8, 512)
                 for cc in range(2):
                     part[u, cc, :, :, columns] = y[:, :, cc].reshape(8, 16, 512).astype(BF16)
@@ -440,23 +411,18 @@
                 arrived(rrx.at[u, way, h, 0], S_RSZ + ((u * 2 + way) * 2 + h) * 5 + 1)
                 value = value + rrx[u, way, h, 0].astype(F32)
             halves.append(value)
-        return jnp.concatenate(
-            [jnp.where(yl == 0, halves[0], halves[1]), jnp.where(yl == 0, halves[1], halves[0])], axis=1
-        )
+        return jnp.concatenate(halves, axis=1)
 
     def between_cross(k):
-        if k == 4:
+        if k == 2:
+            spread_self(1)
+        if k == 1:
             spread_self(2)
-        if k == 3:
-            spread_so(0)
-        if k == 2:
-            spread_self(3)
-        if k == 1:
-            spread_so(1)
 
     both = project_and_sum(0, wo, between_cross)
     ztx[...] = both.astype(BF16)
     send(ztx, zrx, S_RSY, across)
+    spread_so(0)
     arrived(zrx, S_RSY)
     carried = latent_pair + both + zrx[...].astype(F32)
     own_carried = jnp.where(yh == 0, carried[:8], carried[8:])
@@ -464,67 +430,70 @@
     gather_begin(1, carried, gain_s[...])
     for k in range(1, 5):
         gather_step(1, k)
-        if k == 2:
+        if k == 1:
+            spread_self(3)
+        if k == 3:
+            spread_so(1)
             spread_so(2)
-        if k == 3:
-            spread_so(3)
+    spread_so(3)
     gather_end(1)
     spread_self(4)
-
-    qkv = row_projections(1, sqkv)
+    spread_self(5)
+
+    qkv = natural(dot(latent_rows(1), sqkv[...].reshape(D, 3 * HD)), 3 * HD)
     queries = qkv[:, :HD].astype(BF16)
-    k2[0] = qkv[:, HD:2 * HD].astype(BF16)
-    v2[0] = qkv[:, 2 * HD:].T.astype(BF16)
-
-    def later(i):
-        there = {"blk": jnp.minimum(b + i, 7), "grp": g}
-        return (
-            remote(k2.at[0], k2.at[i], S_K2 + i, there),
-            remote(v2.at[0], v2.at[i], S_V2 + i, there),
-        )
-
-    for i in range(1, 8):
-        @pl.when(b + i < 8)
-        def _():
-            for copy in later(i):
-                copy.start()
-
-    def absorb(s, values, top, total, weighted):
-        new = jnp.maximum(top, jnp.max(s, axis=0, keepdims=True))
-        e = jnp.exp(s - new)
-        factor = jnp.exp(top - new)
-        total = total * factor + jnp.sum(e, axis=0, keepdims=True)
-        return new, total, weighted * factor + dot(values, e.astype(BF16))
-
-    s = dot(k2[0], queries, 1, 1) * SCALE
-    s = jnp.where(
-        lax.broadcasted_iota(jnp.int32, (256, 256), 0) <= lax.broadcasted_iota(jnp.int32, (256, 256), 1),
-        s, LOW,
-    )
-    state = absorb(
-        s, v2[0], jnp.full((1, 256), CLIP, F32), jnp.zeros((1, 256), F32), jnp.zeros((HD, 256), F32)
-    )
-
-    def self_block(i, state):
-        arrived(k2.at[i], S_K2 + i)
-        arrived(v2.at[i], S_V2 + i)
-        return absorb(dot(k2[i], queries, 1, 1) * SCALE, v2[i], *state)
-
-    top, total, weighted = lax.fori_loop(1, b + 1, self_block, state)
-    mixed[1] = (weighted / total).T.astype(BF16)
+    kv2[b] = qkv[:, HD:].astype(BF16)
+
+    def spread_keyval(stage):
+        spread(kv2, 0, 256, S_KV2, True, stage)
+
+    def absorb(source, own):
+        block = kv2[source]
+        s = dot(block[:, :HD], queries, 1, 1) * SCALE
+        if own:
+            ids = lax.broadcasted_iota(jnp.int32, (256, 256), 0)
+            s = jnp.where(ids <= lax.broadcasted_iota(jnp.int32, (256, 256), 1), s, LOW)
+        top = jnp.max(s, axis=0, keepdims=True)
+        if not own:
+            top = jnp.maximum(top, top2[...])
+        e = jnp.exp(s - top)
+        total = jnp.sum(e, axis=0, keepdims=True)
+        weighted = dot(block[:, HD:], e.astype(BF16), 0, 0)
+        if not own:
+            factor = jnp.exp(top2[...] - top)
+            total = total + total2[...] * factor
+            weighted = weighted + weighted2[...] * factor
+        top2[...] = top
+        total2[...] = total
+        weighted2[...] = weighted
+
+    def absorb_earlier(*slots):
+        for i in slots:
+            @pl.when(blk_from(i) < b)
+            def _():
+                absorb(blk_from(i), False)
+
+    spread_keyval(0)
+    absorb(b, True)
+    spread_keyval(1)
+    spread_keyval(2)
+    absorb_earlier(4, 1, 3)
+    spread_keyval(3)
+    absorb_earlier(5, 7)
+    spread_keyval(4)
+    absorb_earlier(2)
+    spread_keyval(5)
+    absorb_earlier(6)
+    mixed[1] = (weighted2[...] / total2[...]).T.astype(BF16)
 
     spread_so(4)
+    spread_so(5)
     both = project_and_sum(1, so, lambda k: None)
     ytx[...] = pack_rows(jnp.where(yh == 0, both[8:], both[:8])).astype(BF16)
     send(ytx, yrx, S_RSY + 1, across)
     arrived(yrx, S_RSY + 1)
     out[...] = own_carried + jnp.where(yh == 0, both[:8], both[8:]) + unpack_rows(yrx[...].astype(F32))
 
-    for i in range(1, 8):
-        @pl.when(b + i < 8)
-        def _():
-            for copy in later(i):
-                copy.wait_send()
     for copy in sent:
         copy.wait_send()
 
@@ -544,15 +513,16 @@
         ((1280, HD), BF16),
         ((HD, 1280), BF16),
         ((1024, 2 * HD), F32),
-        ((256, 3 * HD), F32),
         ((1280, 256), F32),
         ((8, HD, 256), BF16),
         ((8, HD, 256), BF16),
         ((8, 8, 256), F32),
         ((8, 8, 256), F32),
         ((2, 256, HD), BF16),
-        ((8, 256, HD), BF16),
-        ((8, HD, 256), BF16),
+        ((8, 256, 2 * HD), BF16),
+        ((1, 256), F32),
+        ((1, 256), F32),
+        ((HD, 256), F32),
         ((16, HALF), BF16),
         ((16, HALF), BF16),
         ((2, 8, 2, 16, D), BF16),

time: 164 us -> 149 us (0.909)
  Pallas kernels: 160 us -> 145 us
    pallas_call x1, Pallas kernels: 160 us -> 145 us  [shards(): pl.pallas_call(layer_kernel, out_shape=jax.ShapeDtypeStruct((8, D), F32),...]
where the time goes in v3:
time: 149 us; the launch traced here: 147 us
  Pallas kernels  145 us (97%)
  local copies, waits for them, and re-layouts  1.57 us (1%)
    pallas_call x1, Pallas kernels, shards(): pl.pallas_call(layer_kernel, out_shape=jax.ShapeDtypeStruct((8, D), F32),...  145 us

profile of v3, /device:TPU:40, one launch (start us, length us, event | category | flops | bytes accessed | tf_op | source)
XLA Modules:
  0.0 146.7 jit_solution(15023858423328160999)
XLA Ops:
  0.0 145.1 %layer.1 = f32[8,4096]{1,0:T(8,128)} custom-call(bf16[1024,4096]{1,0:T(8,128)(2,1)} %prefix.1, bf16[8,4096]{1,0:T(8,128)(2,1)} %latent.1, s32[1,256]{1,0:T(1,128)} %bitcast.7, f32[1,4096]{1,0:T(1,128)} %bitcast.4, f32[1,4096]{1,0:T(1,128)} %bitcast.5, f32[1,4096]{1,0:T(1,128)} %bitcast.6, bf16[512,128]{1,0:T(8,128)(2,1)} %cq.1, bf16[512,128]{1,0:T(8,128)(2,1)} %ck.1, ...), custom_call_target="tpu_custom_call" | custom-call | tf_op jit(solution)/shard_map/layer/pallas_call | solution.py:538
  145.1 1.6 %copy.20 = f32[8,4096]{1,0:T(8,128)} copy(f32[8,4096]{1,0:T(8,128)} %layer.1) | data formatting | bytes 262144

commit v4 on v3

--- a/solution.py
+++ b/solution.py
@@ -36,13 +36,13 @@
 S_Q = _places(8)
 S_O = _places(8)
 S_ST = _places(8)
-S_KV2 = _places(10)
+S_KV2 = _places(4 * 10)
 S_AGY = _places(2)
-S_AGZ = _places(2 * 2 * 5)
-S_AGC = _places(2 * 8)
+S_AGZ = _places(2 * 2 * 5 * 2)
+S_AGC = _places(2 * 8 * 2)
 S_RSC = _places(4)
 S_RSZ = _places(2 * 2 * 2 * 5)
-S_RSY = _places(2)
+S_RSY = _places(4)
 
 
 def rms_rows(values, gain):
@@ -66,9 +66,9 @@
     prefix, latent, limits, gain_p, gain_l, gain_s,
     cq, ck, cv, co, dq, dk, dv, do, sq, sk, sv, so_in,
     out,
-    pre, wqkv, wo, sqkv, so, lim, qn, kn, vt, acc, scores,
+    raw, raw_o, pre, wqkv, wo, sqkv, so, lim, qn, kn, vt, acc, scores,
     otx, orx, sttx, strx, mixed, kv2, top2, total2, weighted2,
-    pk, pkr, gat, part, sib, rtx, rrx, ytx, yrx, ztx, zrx,
+    pk, pkr, gat, part, sib, rtx, rrx, ytx, yrx, ztx, zrx, latent16, carried16,
     ss, rs, ls,
 ):
     b = lax.axis_index("blk")
@@ -117,18 +117,31 @@
         pltpu.make_async_copy(prefix.at[pl.ds(t * 256, 256)], pre.at[pl.ds(t * 256, 256)], ls.at[t])
         for t in range(4)
     ]
+    raw_loads = [
+        pltpu.make_async_copy(source, raw.at[n], ls.at[4 + n])
+        for n, source in enumerate((cq, ck, cv, dq, dk, dv))
+    ] + [
+        pltpu.make_async_copy(source, raw_o.at[n], ls.at[10 + n]) for n, source in enumerate((co, do))
+    ]
+    self_loads = [
+        pltpu.make_async_copy(source, sqkv.at[b, :, pl.ds(n * HD, HD)], ls.at[12 + n])
+        for n, source in enumerate((sq, sk, sv))
+    ] + [pltpu.make_async_copy(so_in, so.at[b], ls.at[15])]
+    for load in raw_loads + self_loads:
+        load.start()
     for load in loads:
         load.start()
 
     def perturbed(weight, delta):
-        return (weight[...].astype(F32) + delta[...].astype(F32)).astype(BF16)
+        return (weight.astype(F32) + delta.astype(F32)).astype(BF16)
 
     rows_l = latent[...].astype(F32)
     pk[...] = pack_rows(rows_l).astype(BF16)
     lim[0] = jnp.broadcast_to(limits[...], (8, 256))
-    wqkv[b, :, :HD] = perturbed(cq, dq)
-    wqkv[b, :, HD:2 * HD] = perturbed(ck, dk)
-    wqkv[b, :, 2 * HD:] = perturbed(cv, dv)
+    for load in raw_loads:
+        load.wait()
+    for n in range(3):
+        wqkv[b, :, n * HD:(n + 1) * HD] = perturbed(raw[n], raw[n + 3])
     pl.semaphore_wait(barrier, 11)
 
     right, left, beside = blk_to(1), blk_to(3), blk_to(4)
@@ -180,7 +193,8 @@
 
     def spread_cross(stage, parts):
         for n in parts:
-            spread(wqkv, n * 128, 128, S_W + 10 * n, n % 2 == 1, stage)
+            start, rows = ((0, 96), (96, 160), (256, 128), (384, 128))[n]
+            spread(wqkv, start, rows, S_W + 10 * n, n % 2 == 1, stage)
 
     def spread_self(stage):
         spread(sqkv, 0, 512, S_SQKV, True, stage)
@@ -194,34 +208,37 @@
     def own_and_other(own, other):
         return jnp.concatenate([jnp.where(yh == 0, own, other), jnp.where(yh == 0, other, own)], axis=0)
 
+    def half_columns(h):
+        return pl.ds(h * HALF, HALF)
+
     def gather_begin(u, rows, gain):
         gat[u, z, c] = rms_rows(rows, gain).astype(BF16)
-        own = gat.at[u, z, c]
-        for way in range(2):
-            send(own, own, S_AGZ + (u * 2 + way) * 5 + 1, vertical[way])
-        send(own, own, S_AGC + u * 8, sibling)
+        for n in range(2):
+            for way in range(2):
+                h = n if way == 0 else 1 - n
+                own = gat.at[u, z, c, :, half_columns(h)]
+                send(own, own, S_AGZ + ((u * 2 + way) * 5 + 1) * 2 + h, vertical[way])
+        for h in range(2):
+            own = gat.at[u, z, c, :, half_columns(h)]
+            send(own, own, S_AGC + u * 16 + h, sibling)
 
     def gather_step(u, k):
-        for way in range(2):
-            zz = (z + 8 - k) % 8 if way == 0 else (z + k) % 8
-            chunk = gat.at[u, zz, c]
-            if k < 4:
-                arrived(chunk, S_AGZ + (u * 2 + way) * 5 + k)
-                onward = chunk
-                if k == 3:
-                    onward = gat.at[u, zz, c, :, pl.ds(way * HALF, HALF)]
-                send(onward, onward, S_AGZ + (u * 2 + way) * 5 + k + 1, vertical[way])
-                send(chunk, chunk, S_AGC + u * 8 + (k if way == 0 else 8 - k), sibling)
-            else:
-                piece = gat.at[u, zz, c, :, pl.ds(way * HALF, HALF)]
-                arrived(piece, S_AGZ + (u * 2 + way) * 5 + 4)
-        if k == 4:
-            chunk = gat.at[u, (z + 4) % 8, c]
-            send(chunk, chunk, S_AGC + u * 8 + 4, sibling)
+        for n in range(2):
+            for way in range(2):
+                h = n if way == 0 else 1 - n
+                if k == 4 and n == 1:
+                    continue
+                zz = (z + 8 - k) % 8 if way == 0 else (z + k) % 8
+                chunk = gat.at[u, zz, c, :, half_columns(h)]
+                arrived(chunk, S_AGZ + ((u * 2 + way) * 5 + k) * 2 + h)
+                if k < 3 or k == 3 and n == 0:
+                    send(chunk, chunk, S_AGZ + ((u * 2 + way) * 5 + k + 1) * 2 + h, vertical[way])
+                send(chunk, chunk, S_AGC + u * 16 + (k if way == 0 else 8 - k) * 2 + h, sibling)
 
     def gather_end(u):
         for k in range(8):
-            arrived(gat.at[u, (z + 8 - k) % 8, 1 - c], S_AGC + u * 8 + k)
+            for h in range(2):
+                arrived(gat.at[u, (z + 8 - k) % 8, 1 - c, :, half_columns(h)], S_AGC + u * 16 + 2 * k + h)
 
     send(pk, pkr, S_AGY, across)
     spread_cross(0, (0, 1, 2, 3))
@@ -257,38 +274,35 @@
 
     norm_prefix(0)
     arrived(pkr, S_AGY)
-    latent_pair = own_and_other(rows_l, unpack_rows(pkr[...].astype(F32)))
-    gather_begin(0, latent_pair, gain_l[...])
+    latent16[...] = own_and_other(rows_l, unpack_rows(pkr[...].astype(F32)))
+    gather_begin(0, latent16[...], gain_l[...])
     norm_prefix(1)
     spread_cross(1, (0, 1))
+    gather_step(0, 1)
     norm_prefix(2)
-    gather_step(0, 1)
+    gather_step(0, 2)
     spread_cross(1, (2, 3))
     norm_prefix(3)
     spread_cross(2, (0, 1))
-    gather_step(0, 2)
     norm_prefix(4)
+    gather_step(0, 3)
     spread_cross(2, (2, 3))
     norm_prefix(5)
-    gather_step(0, 3)
     spread_cross(3, (0, 1))
+    gather_step(0, 4)
     norm_prefix(6)
-    gather_step(0, 4)
     spread_cross(3, (2, 3))
     norm_prefix(7)
-    wo[b] = perturbed(co, do)
-    sqkv[b, :, :HD] = sq[...]
-    sqkv[b, :, HD:2 * HD] = sk[...]
-    sqkv[b, :, 2 * HD:] = sv[...]
-    so[b] = so_in[...]
-    gather_end(0)
+    wo[b] = perturbed(raw_o[0], raw_o[1])
+    spread_wo(0)
     spread_cross(4, (0, 1, 2, 3))
     prefix_part(yl, True)
+    gather_end(0)
     spread_cross(5, (0, 1, 2, 3))
     qn[0] = natural(dot(latent_rows(0), wqkv[:, :, :HD].reshape(D, HD)), HD).astype(BF16)
     for i in range(1, 8):
         send(qn.at[0], qn.at[i], S_Q + i, blk_to(i))
-    spread_wo(0)
+    spread_wo(1)
     prefix_part(1 - yl, False)
     latent_kv = natural(dot(latent_rows(0), wqkv[:, :, HD:].reshape(D, 2 * HD)), 2 * HD)
     for t in range(5):
@@ -339,11 +353,10 @@
 
         return carry
 
-    lax.fori_loop(0, 3, attend, 0)
-    spread_wo(1)
     spread_wo(2)
-    lax.fori_loop(3, 8, attend, 0)
+    lax.fori_loop(0, 7, attend, 0)
     spread_wo(3)
+    lax.fori_loop(7, 8, attend, 0)
     for i in range(1, 8):
         back = {"blk": blk_from(i), "grp": g}
         sent.append(remote(otx.at[i], orx.at[i], S_O + i, back))
@@ -362,14 +375,13 @@
         total = total + factor * strx[i][1:2, :]
         weighted = weighted + orx[i].astype(F32) * factor
     mixed[0] = (weighted / total).T.astype(BF16)
+    for load in self_loads:
+        load.wait()
     spread_self(0)
     spread_wo(4)
     spread_wo(5)
 
-    def half_columns(h):
-        return pl.ds(h * HALF, HALF)
-
-    def project_and_sum(u, weight, between):
+    def project_and_sum(u, weight, between, finish):
         for h in range(2):
             def columns_of(i, carry):
                 columns = pl.ds(pl.multiple_of(i * 512, 512), 512)
@@ -388,54 +400,58 @@
             columns = half_columns(h)
             return part[u, c, zz, :, columns].astype(F32) + sib[u, zz, :, columns].astype(F32)
 
+        def hop(k, way, h, start):
+            if k == start and way == h:
+                arrived(sib.at[u, :, :, half_columns(h)], S_RSC + 2 * u + h)
+            zz = (z + k) % 8 if way == 0 else (z + 8 - k) % 8
+            value = chip_sum(zz, h)
+            at = S_RSZ + ((u * 2 + way) * 2 + h) * 5
+            if k < start:
+                arrived(rrx.at[u, way, h, k], at + k + 1)
+                value = value + rrx[u, way, h, k].astype(F32)
+            rtx[u, way, h, k - 1] = value.astype(BF16)
+            send(rtx.at[u, way, h, k - 1], rrx.at[u, way, h, k - 1], at + k, vertical[way])
+
         for k in (4, 3, 2, 1):
-            for h, way in ((0, 0), (0, 1), (1, 1), (1, 0)):
-                start = 4 if way == h else 3
-                if k == 4 and way == h:
-                    arrived(sib.at[u, :, :, half_columns(h)], S_RSC + 2 * u + h)
-                if k > start:
-                    continue
-                zz = (z + k) % 8 if way == 0 else (z + 8 - k) % 8
-                value = chip_sum(zz, h)
-                at = S_RSZ + ((u * 2 + way) * 2 + h) * 5
-                if k < start:
-                    arrived(rrx.at[u, way, h, k], at + k + 1)
-                    value = value + rrx[u, way, h, k].astype(F32)
-                rtx[u, way, h, k - 1] = value.astype(BF16)
-                send(rtx.at[u, way, h, k - 1], rrx.at[u, way, h, k - 1], at + k, vertical[way])
+            hop(k, 0, 0, 4)
+            hop(k, 1, 1, 4)
+            if k > 1:
+                hop(k - 1, 0, 1, 3)
+                hop(k - 1, 1, 0, 3)
             between(k)
-        halves = []
         for h in range(2):
             value = chip_sum(z, h)
             for way in range(2):
                 arrived(rrx.at[u, way, h, 0], S_RSZ + ((u * 2 + way) * 2 + h) * 5 + 1)
                 value = value + rrx[u, way, h, 0].astype(F32)
-            halves.append(value)
-        return jnp.concatenate(halves, axis=1)
+            finish(h, value)
 
     def between_cross(k):
         if k == 2:
             spread_self(1)
-        if k == 1:
-            spread_self(2)
-
-    both = project_and_sum(0, wo, between_cross)
-    ztx[...] = both.astype(BF16)
-    send(ztx, zrx, S_RSY, across)
+
+    def finish_cross(h, value):
+        columns = half_columns(h)
+        carried16[:, columns] = latent16[:, columns] + value
+        ztx[:, columns] = value.astype(BF16)
+        send(ztx.at[:, columns], zrx.at[:, columns], S_RSY + h, across)
+
+    project_and_sum(0, wo, between_cross, finish_cross)
+    for h in range(2):
+        arrived(zrx.at[:, half_columns(h)], S_RSY + h)
+    spread_self(2)
     spread_so(0)
-    arrived(zrx, S_RSY)
-    carried = latent_pair + both + zrx[...].astype(F32)
+    carried = carried16[...] + zrx[...].astype(F32)
     own_carried = jnp.where(yh == 0, carried[:8], carried[8:])
 
     gather_begin(1, carried, gain_s[...])
     for k in range(1, 5):
         gather_step(1, k)
-        if k == 1:
+        if k == 2:
             spread_self(3)
         if k == 3:
             spread_so(1)
             spread_so(2)
-    spread_so(3)
     gather_end(1)
     spread_self(4)
     spread_self(5)
@@ -445,7 +461,8 @@
     kv2[b] = qkv[:, HD:].astype(BF16)
 
     def spread_keyval(stage):
-        spread(kv2, 0, 256, S_KV2, True, stage)
+        for n in range(4):
+            spread(kv2, n * 64, 64, S_KV2 + 10 * n, n % 2 == 1, stage)
 
     def absorb(source, own):
         block = kv2[source]
@@ -474,25 +491,30 @@
                 absorb(blk_from(i), False)
 
     spread_keyval(0)
+    spread_so(3)
     absorb(b, True)
     spread_keyval(1)
     spread_keyval(2)
-    absorb_earlier(4, 1, 3)
     spread_keyval(3)
-    absorb_earlier(5, 7)
     spread_keyval(4)
-    absorb_earlier(2)
+    absorb_earlier(1, 3, 2)
     spread_keyval(5)
-    absorb_earlier(6)
+    absorb_earlier(4, 5, 7, 6)
     mixed[1] = (weighted2[...] / total2[...]).T.astype(BF16)
 
     spread_so(4)
     spread_so(5)
-    both = project_and_sum(1, so, lambda k: None)
-    ytx[...] = pack_rows(jnp.where(yh == 0, both[8:], both[:8])).astype(BF16)
-    send(ytx, yrx, S_RSY + 1, across)
-    arrived(yrx, S_RSY + 1)
-    out[...] = own_carried + jnp.where(yh == 0, both[:8], both[8:]) + unpack_rows(yrx[...].astype(F32))
+    def finish_self(h, value):
+        columns = half_columns(h)
+        out[:, columns] = own_carried[:, columns.start:columns.start + HALF] + jnp.where(yh == 0, value[:8], value[8:])
+        ytx[:, columns] = jnp.where(yh == 0, value[8:], value[:8])
+        send(ytx.at[:, columns], yrx.at[:, columns], S_RSY + 2 + h, across)
+
+    project_and_sum(1, so, lambda k: None, finish_self)
+    for h in range(2):
+        columns = half_columns(h)
+        arrived(yrx.at[:, columns], S_RSY + 2 + h)
+        out[:, columns] = out[:, columns] + yrx[:, columns]
 
     for copy in sent:
         copy.wait_send()
@@ -503,6 +525,8 @@
     vmem = pl.BlockSpec(memory_space=pltpu.VMEM)
     sem = pltpu.SemaphoreType.DMA
     scratch = [
+        ((6, 512, HD), BF16),
+        ((2, HD, 512), BF16),
         ((1024, D), BF16),
         ((8, 512, 3 * HD), BF16),
         ((8, HD, 512), BF16),
@@ -530,18 +554,21 @@
         ((2, 8, 16, D), BF16),
         ((2, 2, 2, 4, 16, HALF), BF16),
         ((2, 2, 2, 4, 16, HALF), BF16),
-        ((16, HALF), BF16),
-        ((16, HALF), BF16),
+        ((8, D), F32),
+        ((8, D), F32),
         ((16, D), BF16),
         ((16, D), BF16),
+        ((16, D), F32),
+        ((16, D), F32),
     ]
     return pl.pallas_call(
         layer_kernel,
         out_shape=jax.ShapeDtypeStruct((8, D), F32),
-        in_specs=[pl.BlockSpec(memory_space=pl.ANY)] + [vmem] * 17,
+        in_specs=[pl.BlockSpec(memory_space=pl.ANY)] + [vmem] * 5
+        + [pl.BlockSpec(memory_space=pl.ANY)] * 12,
         out_specs=vmem,
         scratch_shapes=[pltpu.VMEM(shape, dtype) for shape, dtype in scratch]
-        + [sem((N_SEM,)), sem((N_SEM,)), sem((4,))],
+        + [sem((N_SEM,)), sem((N_SEM,)), sem((16,))],
         compiler_params=pltpu.CompilerParams(
             collective_id=0, has_side_effects=True, vmem_limit_bytes=56 * 1024 * 1024
         ),

time: 149 us -> 137 us (0.919)
  Pallas kernels: 145 us -> 134 us
    pallas_call x1, Pallas kernels: 145 us -> 134 us  [shards(): pl.pallas_call(layer_kernel, out_shape=jax.ShapeDtypeStruct((8, D), F32),...]
where the time goes in v4:
time: 137 us; the launch traced here: 135 us
  Pallas kernels  134 us (98%)
  local copies, waits for them, and re-layouts  1.57 us (1%)
    pallas_call x1, Pallas kernels, shards(): pl.pallas_call(layer_kernel, out_shape=jax.ShapeDtypeStruct((8, D), F32),...  134 us

profile of v4, /device:TPU:40, one launch (start us, length us, event | category | flops | bytes accessed | tf_op | source)
XLA Modules:
  0.0 135.5 jit_solution(1580752173505019799)
XLA Ops:
  0.0 133.9 %layer.1 = f32[8,4096]{1,0:T(8,128)} custom-call(bf16[1024,4096]{1,0:T(8,128)(2,1)} %prefix.1, bf16[8,4096]{1,0:T(8,128)(2,1)} %latent.1, s32[1,256]{1,0:T(1,128)} %bitcast.7, f32[1,4096]{1,0:T(1,128)} %bitcast.4, f32[1,4096]{1,0:T(1,128)} %bitcast.5, f32[1,4096]{1,0:T(1,128)} %bitcast.6, bf16[512,128]{1,0:T(8,128)(2,1)} %cq.1, bf16[512,128]{1,0:T(8,128)(2,1)} %ck.1, ...), custom_call_target="tpu_custom_call" | custom-call | tf_op jit(solution)/shard_map/layer/pallas_call | solution.py:564
  133.9 1.6 %copy.20 = f32[8,4096]{1,0:T(8,128)} copy(f32[8,4096]{1,0:T(8,128)} %layer.1) | data formatting | bytes 262144

commit v5 on v4

--- a/solution.py
+++ b/solution.py
@@ -51,7 +51,8 @@
 
 
 def pack_rows(rows):
-    return jnp.concatenate([rows[:, :HALF], rows[:, HALF:]], axis=0)
+    half = rows.shape[1] // 2
+    return jnp.concatenate([rows[:, :half], rows[:, half:]], axis=0)
 
 
 def unpack_rows(packed):
@@ -235,8 +236,8 @@
                     send(chunk, chunk, S_AGZ + ((u * 2 + way) * 5 + k + 1) * 2 + h, vertical[way])
                 send(chunk, chunk, S_AGC + u * 16 + (k if way == 0 else 8 - k) * 2 + h, sibling)
 
-    def gather_end(u):
-        for k in range(8):
+    def gather_end(u, places):
+        for k in places:
             for h in range(2):
                 arrived(gat.at[u, (z + 8 - k) % 8, 1 - c, :, half_columns(h)], S_AGC + u * 16 + 2 * k + h)
 
@@ -268,9 +269,9 @@
         return gat[u].reshape(256, D)
 
     def natural(values, width):
-        cut = values.reshape(8, 2, 2, 8, width)
+        cut = values.reshape(-1, 2, 2, 8, width)
         order = jnp.stack([cut[:, cc, yy] for yy in range(2) for cc in range(2)], axis=1)
-        return order.reshape(256, width)
+        return order.reshape(values.shape[0], width)
 
     norm_prefix(0)
     arrived(pkr, S_AGY)
@@ -297,10 +298,10 @@
     spread_wo(0)
     spread_cross(4, (0, 1, 2, 3))
     prefix_part(yl, True)
-    gather_end(0)
+    gather_end(0, range(8))
     spread_cross(5, (0, 1, 2, 3))
     qn[0] = natural(dot(latent_rows(0), wqkv[:, :, :HD].reshape(D, HD)), HD).astype(BF16)
-    for i in range(1, 8):
+    for i in (4, 5, 7, 6, 1, 3, 2):
         send(qn.at[0], qn.at[i], S_Q + i, blk_to(i))
     spread_wo(1)
     prefix_part(1 - yl, False)
@@ -311,14 +312,7 @@
         kn[rows, :] = values[:, :HD].astype(BF16)
         vt[:, rows] = values[:, HD:].T.astype(BF16)
 
-    def attend(n, carry):
-        i = (n + 1) % 8
-
-        @pl.when(i > 0)
-        def _():
-            arrived(qn.at[i], S_Q + i)
-            arrived(lim.at[i], S_LIM + i)
-
+    def attend(i):
         source = blk_from(i)
         queries = qn[i]
         seen = lim[i][0:1, :]
@@ -340,37 +334,79 @@
             e = jnp.exp(scores[pl.ds(t * 256, 256), :] - top)
             total = total + jnp.sum(e.reshape(32, 8, 256), axis=0)
             weighted = weighted + dot(vt[:, pl.ds(t * 256, 256)], e.astype(BF16))
-        total = jnp.sum(total, axis=0, keepdims=True)
+        return top, jnp.sum(total, axis=0, keepdims=True), weighted
+
+    def keep(i, top, total, weighted):
         otx[i] = weighted.astype(BF16)
-        first = lax.broadcasted_iota(jnp.int32, (8, 256), 0) == 0
+        first = lax.broadcasted_iota(jnp.int32, (2, 256), 0) == 0
         sttx[i] = jnp.where(first, top, total)
+
+    def across_copies(i):
+        return (
+            remote(otx.at[i], orx.at[i], S_O + i, beside),
+            remote(sttx.at[i], strx.at[i], S_ST + i, beside),
+        )
+
+    def along_copies(i):
+        back = {"blk": blk_from(i), "grp": g}
+        return (
+            remote(otx.at[i], orx.at[i], S_O + i, back),
+            remote(sttx.at[i], strx.at[i], S_ST + i, back),
+        )
+
+    def attend_partner_row(n, carry):
+        i = n + 4
+        arrived(lim.at[i], S_LIM + i)
+        arrived(qn.at[i], S_Q + i)
+        keep(i, *attend(i))
+        for copy in across_copies(i):
+            copy.start()
+        return carry
+
+    def attend_own_row(n, carry):
+        i = (n + 1) % 4
 
         @pl.when(i > 0)
         def _():
-            back = {"blk": source, "grp": g}
-            remote(otx.at[i], orx.at[i], S_O + i, back).start()
-            remote(sttx.at[i], strx.at[i], S_ST + i, back).start()
+            arrived(lim.at[i], S_LIM + i)
+            arrived(qn.at[i], S_Q + i)
+
+        top, total, weighted = attend(i)
+        arrived(orx.at[i + 4], S_O + i + 4)
+        arrived(strx.at[i + 4], S_ST + i + 4)
+        top_there = strx[i + 4][0:1, :]
+        both = jnp.maximum(top, top_there)
+        here_part, there_part = jnp.exp(top - both), jnp.exp(top_there - both)
+        keep(
+            i, both, total * here_part + strx[i + 4][1:2, :] * there_part,
+            weighted * here_part + orx[i + 4].astype(F32) * there_part,
+        )
+
+        @pl.when(i > 0)
+        def _():
+            for copy in along_copies(i):
+                copy.start()
 
         return carry
 
     spread_wo(2)
-    lax.fori_loop(0, 7, attend, 0)
+    lax.fori_loop(0, 4, attend_partner_row, 0)
+    lax.fori_loop(0, 3, attend_own_row, 0)
     spread_wo(3)
-    lax.fori_loop(7, 8, attend, 0)
+    lax.fori_loop(3, 4, attend_own_row, 0)
     for i in range(1, 8):
-        back = {"blk": blk_from(i), "grp": g}
-        sent.append(remote(otx.at[i], orx.at[i], S_O + i, back))
-        sent.append(remote(sttx.at[i], strx.at[i], S_ST + i, back))
+        sent.extend(along_copies(i) if i < 4 else across_copies(i))
+
     orx[0] = otx[0]
     strx[0] = sttx[0]
-    for i in range(1, 8):
+    for i in range(1, 4):
         arrived(orx.at[i], S_O + i)
         arrived(strx.at[i], S_ST + i)
-    tops = [strx[i][0:1, :] for i in range(8)]
+    tops = [strx[i][0:1, :] for i in range(4)]
     top = functools.reduce(jnp.maximum, tops)
     total = jnp.zeros((1, 256), F32)
     weighted = jnp.zeros((HD, 256), F32)
-    for i in range(8):
+    for i in range(4):
         factor = jnp.exp(tops[i] - top)
         total = total + factor * strx[i][1:2, :]
         weighted = weighted + orx[i].astype(F32) * factor
@@ -427,8 +463,10 @@
             finish(h, value)
 
     def between_cross(k):
-        if k == 2:
+        if k == 3:
             spread_self(1)
+        if k == 1:
+            spread_self(2)
 
     def finish_cross(h, value):
         columns = half_columns(h)
@@ -439,36 +477,51 @@
     project_and_sum(0, wo, between_cross, finish_cross)
     for h in range(2):
         arrived(zrx.at[:, half_columns(h)], S_RSY + h)
-    spread_self(2)
-    spread_so(0)
     carried = carried16[...] + zrx[...].astype(F32)
     own_carried = jnp.where(yh == 0, carried[:8], carried[8:])
 
     gather_begin(1, carried, gain_s[...])
-    for k in range(1, 5):
-        gather_step(1, k)
-        if k == 2:
-            spread_self(3)
-        if k == 3:
-            spread_so(1)
-            spread_so(2)
-    gather_end(1)
+    spread_self(3)
+    spread_so(0)
+
+    def arrived_rows(places):
+        return jnp.concatenate([gat[1, (z + 8 - k) % 8].reshape(32, D) for k in places], axis=0)
+
+    def keyval(places, start):
+        rows = natural(dot(arrived_rows(places), sqkv[:, :, HD:].reshape(D, 2 * HD)), 2 * HD)
+        kv2[b, pl.ds(start, 32 * len(places))] = rows.astype(BF16)
+
+    def spread_keyval(stage, parts):
+        for n in parts:
+            start, rows = ((0, 64), (64, 96), (160, 32), (192, 64))[n]
+            spread(kv2, start, rows, S_KV2 + 10 * n, n % 2 == 1, stage)
+
+    near, far = (0, 1, 7, 2, 6), (3, 5, 4)
+    gather_step(1, 1)
+    gather_step(1, 2)
+    spread_so(1)
+    gather_step(1, 3)
     spread_self(4)
     spread_self(5)
-
-    qkv = natural(dot(latent_rows(1), sqkv[...].reshape(D, 3 * HD)), 3 * HD)
-    queries = qkv[:, :HD].astype(BF16)
-    kv2[b] = qkv[:, HD:].astype(BF16)
-
-    def spread_keyval(stage):
-        for n in range(4):
-            spread(kv2, n * 64, 64, S_KV2 + 10 * n, n % 2 == 1, stage)
+    gather_end(1, near)
+    keyval(near, 0)
+    spread_keyval(0, (0, 1))
+    gather_step(1, 4)
+    gather_end(1, far)
+    keyval(far, 160)
+    spread_keyval(0, (2, 3))
+    spread_keyval(1, (0, 1))
+    spread_so(2)
+    queries = natural(dot(latent_rows(1), sqkv[:, :, :HD].reshape(D, HD)), HD).astype(BF16)
 
     def absorb(source, own):
         block = kv2[source]
         s = dot(block[:, :HD], queries, 1, 1) * SCALE
         if own:
-            ids = lax.broadcasted_iota(jnp.int32, (256, 256), 0)
+            row = lax.broadcasted_iota(jnp.int32, (256, 256), 0)
+            place = row >> 5
+            distance = (place + 1) >> 1
+            ids = ((z + 8 + jnp.where((place & 1) == 1, -distance, distance)) & 7) * 32 + (row & 31)
             s = jnp.where(ids <= lax.broadcasted_iota(jnp.int32, (256, 256), 1), s, LOW)
         top = jnp.max(s, axis=0, keepdims=True)
         if not own:
@@ -490,15 +543,16 @@
             def _():
                 absorb(blk_from(i), False)
 
-    spread_keyval(0)
+    absorb(b, True)
+    spread_keyval(2, (0, 1))
+    spread_keyval(1, (2, 3))
+    spread_keyval(3, (0, 1))
+    spread_keyval(2, (2, 3))
     spread_so(3)
-    absorb(b, True)
-    spread_keyval(1)
-    spread_keyval(2)
-    spread_keyval(3)
-    spread_keyval(4)
+    spread_keyval(3, (2, 3))
+    spread_keyval(4, range(4))
     absorb_earlier(1, 3, 2)
-    spread_keyval(5)
+    spread_keyval(5, range(4))
     absorb_earlier(4, 5, 7, 6)
     mixed[1] = (weighted2[...] / total2[...]).T.astype(BF16)
 
@@ -507,14 +561,14 @@
     def finish_self(h, value):
         columns = half_columns(h)
         out[:, columns] = own_carried[:, columns.start:columns.start + HALF] + jnp.where(yh == 0, value[:8], value[8:])
-        ytx[:, columns] = jnp.where(yh == 0, value[8:], value[:8])
-        send(ytx.at[:, columns], yrx.at[:, columns], S_RSY + 2 + h, across)
+        ytx[h] = pack_rows(jnp.where(yh == 0, value[8:], value[:8])).astype(BF16)
+        send(ytx.at[h], yrx.at[h], S_RSY + 2 + h, across)
 
     project_and_sum(1, so, lambda k: None, finish_self)
     for h in range(2):
         columns = half_columns(h)
-        arrived(yrx.at[:, columns], S_RSY + 2 + h)
-        out[:, columns] = out[:, columns] + yrx[:, columns]
+        arrived(yrx.at[h], S_RSY + 2 + h)
+        out[:, columns] = out[:, columns] + unpack_rows(yrx[h].astype(F32))
 
     for copy in sent:
         copy.wait_send()
@@ -540,8 +594,8 @@
         ((1280, 256), F32),
         ((8, HD, 256), BF16),
         ((8, HD, 256), BF16),
-        ((8, 8, 256), F32),
-        ((8, 8, 256), F32),
+        ((8, 2, 256), F32),
+        ((8, 2, 256), F32),
         ((2, 256, HD), BF16),
         ((8, 256, 2 * HD), BF16),
         ((1, 256), F32),
@@ -554,8 +608,8 @@
         ((2, 8, 16, D), BF16),
         ((2, 2, 2, 4, 16, HALF), BF16),
         ((2, 2, 2, 4, 16, HALF), BF16),
-        ((8, D), F32),
-        ((8, D), F32),
+        ((2, 16, HALF // 2), BF16),
+        ((2, 16, HALF // 2), BF16),
         ((16, D), BF16),
         ((16, D), BF16),
         ((16, D), F32),

time: 137 us -> 134 us (0.978)
  Pallas kernels: 134 us -> 131 us
    pallas_call x1, Pallas kernels: 134 us -> 131 us  [shards(): pl.pallas_call(layer_kernel, out_shape=jax.ShapeDtypeStruct((8, D), F32),...]
where the time goes in v5:
time: 134 us; the launch traced here: 133 us
  Pallas kernels  131 us (98%)
  local copies, waits for them, and re-layouts  1.57 us (1%)
    pallas_call x1, Pallas kernels, shards(): pl.pallas_call(layer_kernel, out_shape=jax.ShapeDtypeStruct((8, D), F32),...  131 us

profile of v5, /device:TPU:40, one launch (start us, length us, event | category | flops | bytes accessed | tf_op | source)
XLA Modules:
  0.0 133.0 jit_solution(13511388604149111593)
XLA Ops:
  0.0 131.4 %layer.1 = f32[8,4096]{1,0:T(8,128)} custom-call(bf16[1024,4096]{1,0:T(8,128)(2,1)} %prefix.1, bf16[8,4096]{1,0:T(8,128)(2,1)} %latent.1, s32[1,256]{1,0:T(1,128)} %bitcast.7, f32[1,4096]{1,0:T(1,128)} %bitcast.4, f32[1,4096]{1,0:T(1,128)} %bitcast.5, f32[1,4096]{1,0:T(1,128)} %bitcast.6, bf16[512,128]{1,0:T(8,128)(2,1)} %cq.1, bf16[512,128]{1,0:T(8,128)(2,1)} %ck.1, ...), custom_call_target="tpu_custom_call" | custom-call | tf_op jit(solution)/shard_map/layer/pallas_call | solution.py:618
  131.4 1.6 %copy.20 = f32[8,4096]{1,0:T(8,128)} copy(f32[8,4096]{1,0:T(8,128)} %layer.1) | data formatting | bytes 262144

commit v6 on v5

--- a/solution.py
+++ b/solution.py
@@ -1,4 +1,5 @@
 import functools
+import math
 
 import jax
 import jax.numpy as jnp
@@ -28,21 +29,24 @@
     return first
 
 
-S_W = _places(4 * 10)
-S_WO = _places(10)
-S_SQKV = _places(10)
-S_SO = _places(10)
-S_LIM = _places(8)
-S_Q = _places(8)
-S_O = _places(8)
-S_ST = _places(8)
-S_KV2 = _places(4 * 10)
-S_AGY = _places(2)
-S_AGZ = _places(2 * 2 * 5 * 2)
-S_AGC = _places(2 * 8 * 2)
+S_W = _places(4 * 7) - 1
+S_WO = _places(7) - 1
+S_SQKV = _places(7) - 1
+S_SO = _places(7) - 1
+S_LIM = _places(1)
+S_Q = _places(7) - 1
+S_O = _places(7) - 1
+S_ST = _places(7) - 1
+S_KV2 = _places(4 * 7) - 1
+S_AGY = _places(1)
+S_AGZ = _places(2 * 2 * 7)
+S_AGC = _places(3)
 S_RSC = _places(4)
-S_RSZ = _places(2 * 2 * 2 * 5)
+S_RSZ = _places(2 * 2 * 2 * 4) - 1
 S_RSY = _places(4)
+
+GROUP_KIB = 1100
+N_GROUPS = 18
 
 
 def rms_rows(values, gain):
@@ -92,18 +96,23 @@
     below = grp_at((z + 7) % 8, yh, c)
     vertical = (above, below)
 
-    def remote(src, dst, place, device):
+    def remote(src, dst, place, device, group=0):
         return pltpu.make_async_remote_copy(
-            src_ref=src, dst_ref=dst, send_sem=ss.at[place], recv_sem=rs.at[place],
+            src_ref=src, dst_ref=dst, send_sem=ss.at[group], recv_sem=rs.at[place],
             device_id=device, device_id_type=MESH,
         )
 
-    sent = []
+    sent_kib = [0]
+
+    def group_for(src, count=1):
+        kib = count * math.prod(src.shape) * jnp.dtype(src.dtype).itemsize // 1024
+        if sent_kib[-1] + kib > GROUP_KIB and sent_kib[-1] % 8 == 0:
+            sent_kib.append(0)
+        sent_kib[-1] += kib
+        return len(sent_kib) - 1
 
     def send(src, dst, place, device):
-        copy = remote(src, dst, place, device)
-        copy.start()
-        sent.append(copy)
+        remote(src, dst, place, device, group_for(src)).start()
 
     def arrived(dst, place):
         remote(dst, dst, place, sibling).wait_recv()
@@ -119,15 +128,14 @@
         for t in range(4)
     ]
     raw_loads = [
-        pltpu.make_async_copy(source, raw.at[n], ls.at[4 + n])
-        for n, source in enumerate((cq, ck, cv, dq, dk, dv))
+        pltpu.make_async_copy(source, raw.at[n], ls.at[4]) for n, source in enumerate((cq, ck, cv, dq, dk, dv))
     ] + [
-        pltpu.make_async_copy(source, raw_o.at[n], ls.at[10 + n]) for n, source in enumerate((co, do))
+        pltpu.make_async_copy(source, raw_o.at[n], ls.at[5]) for n, source in enumerate((co, do))
     ]
     self_loads = [
-        pltpu.make_async_copy(source, sqkv.at[b, :, pl.ds(n * HD, HD)], ls.at[12 + n])
+        pltpu.make_async_copy(source, sqkv.at[b, :, pl.ds(n * HD, HD)], ls.at[6])
         for n, source in enumerate((sq, sk, sv))
-    ] + [pltpu.make_async_copy(so_in, so.at[b], ls.at[15])]
+    ] + [pltpu.make_async_copy(so_in, so.at[b], ls.at[7])]
     for load in raw_loads + self_loads:
         load.start()
     for load in loads:
@@ -139,8 +147,7 @@
     rows_l = latent[...].astype(F32)
     pk[...] = pack_rows(rows_l).astype(BF16)
     lim[0] = jnp.broadcast_to(limits[...], (8, 256))
-    for load in raw_loads:
-        load.wait()
+    pltpu.make_async_copy(raw, raw, ls.at[4]).wait()
     for n in range(3):
         wqkv[b, :, n * HD:(n + 1) * HD] = perturbed(raw[n], raw[n + 3])
     pl.semaphore_wait(barrier, 11)
@@ -165,28 +172,25 @@
             arrived(here(1), place + 1)
             send(here(1, 0), here(1, 0), place + 2, right)
             arrived(here(3), place + 3)
-            send(here(3, 1), here(3, 1), place + 8, left)
+            send(here(3, 1), here(3, 1), place + 2, left)
         elif y_first and stage == 3:
             arrived(here(5), place + 5)
             send(here(5, 0), here(5, 0), place + 6, right)
             arrived(here(7), place + 7)
-            send(here(7, 1), here(7, 1), place + 9, left)
+            send(here(7, 1), here(7, 1), place + 6, left)
         elif y_first and stage == 4:
-            arrived(here(2, 0), place + 2)
-            arrived(here(2, 1), place + 8)
+            arrived(here(2), place + 2)
         elif y_first:
-            arrived(here(6, 0), place + 6)
-            arrived(here(6, 1), place + 9)
+            arrived(here(6), place + 6)
         elif stage == 1:
             arrived(here(1), place + 1)
             send(here(1, 0), here(1, 0), place + 2, right)
             send(here(1), here(1), place + 5, beside)
             arrived(here(3), place + 3)
-            send(here(3, 1), here(3, 1), place + 8, left)
+            send(here(3, 1), here(3, 1), place + 2, left)
             send(here(3), here(3), place + 7, beside)
         elif stage == 2:
-            arrived(here(2, 0), place + 2)
-            arrived(here(2, 1), place + 8)
+            arrived(here(2), place + 2)
             send(here(2), here(2), place + 6, beside)
         elif stage == 5:
             for i in (4, 5, 7, 6):
@@ -195,7 +199,7 @@
     def spread_cross(stage, parts):
         for n in parts:
             start, rows = ((0, 96), (96, 160), (256, 128), (384, 128))[n]
-            spread(wqkv, start, rows, S_W + 10 * n, n % 2 == 1, stage)
+            spread(wqkv, start, rows, S_W + 7 * n, n % 2 == 1, stage)
 
     def spread_self(stage):
         spread(sqkv, 0, 512, S_SQKV, True, stage)
@@ -211,6 +215,12 @@
 
     def half_columns(h):
         return pl.ds(h * HALF, HALF)
+
+    def agz(u, way, k, h):
+        return S_AGZ + (u * 2 + way) * 7 + (k - 1) * 2 + (h if k < 4 else 0)
+
+    def agc(u, place):
+        return S_AGC + (u if place not in (3, 4, 5) else 2 * u)
 
     def gather_begin(u, rows, gain):
         gat[u, z, c] = rms_rows(rows, gain).astype(BF16)
@@ -218,10 +228,10 @@
             for way in range(2):
                 h = n if way == 0 else 1 - n
                 own = gat.at[u, z, c, :, half_columns(h)]
-                send(own, own, S_AGZ + ((u * 2 + way) * 5 + 1) * 2 + h, vertical[way])
+                send(own, own, agz(u, way, 1, h), vertical[way])
         for h in range(2):
             own = gat.at[u, z, c, :, half_columns(h)]
-            send(own, own, S_AGC + u * 16 + h, sibling)
+            send(own, own, agc(u, 0), sibling)
 
     def gather_step(u, k):
         for n in range(2):
@@ -231,20 +241,18 @@
                     continue
                 zz = (z + 8 - k) % 8 if way == 0 else (z + k) % 8
                 chunk = gat.at[u, zz, c, :, half_columns(h)]
-                arrived(chunk, S_AGZ + ((u * 2 + way) * 5 + k) * 2 + h)
+                arrived(chunk, agz(u, way, k, h))
                 if k < 3 or k == 3 and n == 0:
-                    send(chunk, chunk, S_AGZ + ((u * 2 + way) * 5 + k + 1) * 2 + h, vertical[way])
-                send(chunk, chunk, S_AGC + u * 16 + (k if way == 0 else 8 - k) * 2 + h, sibling)
+                    send(chunk, chunk, agz(u, way, k + 1, h), vertical[way])
+                send(chunk, chunk, agc(u, k if way == 0 else 8 - k), sibling)
 
     def gather_end(u, places):
-        for k in places:
-            for h in range(2):
-                arrived(gat.at[u, (z + 8 - k) % 8, 1 - c, :, half_columns(h)], S_AGC + u * 16 + 2 * k + h)
+        arrived(gat.at[u, pl.ds(0, len(places)), 1 - c], agc(u, places[0]))
 
     send(pk, pkr, S_AGY, across)
     spread_cross(0, (0, 1, 2, 3))
     for i in range(1, 8):
-        send(lim.at[0], lim.at[i], S_LIM + i, blk_to(i))
+        send(lim.at[0], lim.at[i], S_LIM, blk_to(i))
 
     def norm_prefix(t):
         if t % 2 == 0:
@@ -294,6 +302,7 @@
     norm_prefix(6)
     spread_cross(3, (2, 3))
     norm_prefix(7)
+    pltpu.make_async_copy(raw_o, raw_o, ls.at[5]).wait()
     wo[b] = perturbed(raw_o[0], raw_o[1])
     spread_wo(0)
     spread_cross(4, (0, 1, 2, 3))
@@ -303,8 +312,8 @@
     qn[0] = natural(dot(latent_rows(0), wqkv[:, :, :HD].reshape(D, HD)), HD).astype(BF16)
     for i in (4, 5, 7, 6, 1, 3, 2):
         send(qn.at[0], qn.at[i], S_Q + i, blk_to(i))
+    prefix_part(1 - yl, False)
     spread_wo(1)
-    prefix_part(1 - yl, False)
     latent_kv = natural(dot(latent_rows(0), wqkv[:, :, HD:].reshape(D, 2 * HD)), 2 * HD)
     for t in range(5):
         rows = pl.ds(t * 256, 256)
@@ -341,22 +350,23 @@
         first = lax.broadcasted_iota(jnp.int32, (2, 256), 0) == 0
         sttx[i] = jnp.where(first, top, total)
 
+    output_group = group_for(otx.at[0], 7)
+
     def across_copies(i):
         return (
-            remote(otx.at[i], orx.at[i], S_O + i, beside),
-            remote(sttx.at[i], strx.at[i], S_ST + i, beside),
+            remote(otx.at[i], orx.at[i], S_O + i, beside, output_group),
+            remote(sttx.at[i], strx.at[i], S_ST + i, beside, N_GROUPS - 1),
         )
 
     def along_copies(i):
         back = {"blk": blk_from(i), "grp": g}
         return (
-            remote(otx.at[i], orx.at[i], S_O + i, back),
-            remote(sttx.at[i], strx.at[i], S_ST + i, back),
+            remote(otx.at[i], orx.at[i], S_O + i, back, output_group),
+            remote(sttx.at[i], strx.at[i], S_ST + i, back, N_GROUPS - 1),
         )
 
     def attend_partner_row(n, carry):
         i = n + 4
-        arrived(lim.at[i], S_LIM + i)
         arrived(qn.at[i], S_Q + i)
         keep(i, *attend(i))
         for copy in across_copies(i):
@@ -368,7 +378,6 @@
 
         @pl.when(i > 0)
         def _():
-            arrived(lim.at[i], S_LIM + i)
             arrived(qn.at[i], S_Q + i)
 
         top, total, weighted = attend(i)
@@ -390,13 +399,11 @@
         return carry
 
     spread_wo(2)
+    arrived(lim.at[pl.ds(1, 7)], S_LIM)
     lax.fori_loop(0, 4, attend_partner_row, 0)
     lax.fori_loop(0, 3, attend_own_row, 0)
     spread_wo(3)
     lax.fori_loop(3, 4, attend_own_row, 0)
-    for i in range(1, 8):
-        sent.extend(along_copies(i) if i < 4 else across_copies(i))
-
     orx[0] = otx[0]
     strx[0] = sttx[0]
     for i in range(1, 4):
@@ -411,8 +418,8 @@
         total = total + factor * strx[i][1:2, :]
         weighted = weighted + orx[i].astype(F32) * factor
     mixed[0] = (weighted / total).T.astype(BF16)
-    for load in self_loads:
-        load.wait()
+    pltpu.make_async_copy(sqkv.at[b], sqkv.at[b], ls.at[6]).wait()
+    self_loads[3].wait()
     spread_self(0)
     spread_wo(4)
     spread_wo(5)
@@ -441,7 +448,7 @@
                 arrived(sib.at[u, :, :, half_columns(h)], S_RSC + 2 * u + h)
             zz = (z + k) % 8 if way == 0 else (z + 8 - k) % 8
             value = chip_sum(zz, h)
-            at = S_RSZ + ((u * 2 + way) * 2 + h) * 5
+            at = S_RSZ + ((u * 2 + way) * 2 + h) * 4
             if k < start:
                 arrived(rrx.at[u, way, h, k], at + k + 1)
                 value = value + rrx[u, way, h, k].astype(F32)
@@ -458,7 +465,7 @@
         for h in range(2):
             value = chip_sum(z, h)
             for way in range(2):
-                arrived(rrx.at[u, way, h, 0], S_RSZ + ((u * 2 + way) * 2 + h) * 5 + 1)
+                arrived(rrx.at[u, way, h, 0], S_RSZ + ((u * 2 + way) * 2 + h) * 4 + 1)
                 value = value + rrx[u, way, h, 0].astype(F32)
             finish(h, value)
 
@@ -494,7 +501,7 @@
     def spread_keyval(stage, parts):
         for n in parts:
             start, rows = ((0, 64), (64, 96), (160, 32), (192, 64))[n]
-            spread(kv2, start, rows, S_KV2 + 10 * n, n % 2 == 1, stage)
+            spread(kv2, start, rows, S_KV2 + 7 * n, n % 2 == 1, stage)
 
     near, far = (0, 1, 7, 2, 6), (3, 5, 4)
     gather_step(1, 1)
@@ -570,8 +577,10 @@
         arrived(yrx.at[h], S_RSY + 2 + h)
         out[:, columns] = out[:, columns] + unpack_rows(yrx[h].astype(F32))
 
-    for copy in sent:
-        copy.wait_send()
+    for group, kib in enumerate(sent_kib):
+        everything = scores.at[pl.ds(0, kib)]
+        remote(everything, everything, 0, sibling, group).wait_send()
+    remote(sttx.at[pl.ds(0, 7)], strx.at[pl.ds(0, 7)], 0, sibling, N_GROUPS - 1).wait_send()
 
 
 def shards(*arguments):
@@ -622,7 +631,7 @@
         + [pl.BlockSpec(memory_space=pl.ANY)] * 12,
         out_specs=vmem,
         scratch_shapes=[pltpu.VMEM(shape, dtype) for shape, dtype in scratch]
-        + [sem((N_SEM,)), sem((N_SEM,)), sem((16,))],
+        + [sem((N_GROUPS,)), sem((N_SEM,)), sem((8,))],
         compiler_params=pltpu.CompilerParams(
             collective_id=0, has_side_effects=True, vmem_limit_bytes=56 * 1024 * 1024
         ),

time: 134 us -> 130 us (0.970)
  Pallas kernels: 131 us -> 128 us
    pallas_call x1, Pallas kernels: 131 us -> 128 us  [shards(): pl.pallas_call(layer_kernel, out_shape=jax.ShapeDtypeStruct((8, D), F32),...]
where the time goes in v6:
time: 130 us; the launch traced here: 129 us
  Pallas kernels  128 us (98%)
  local copies, waits for them, and re-layouts  1.57 us (1%)
    pallas_call x1, Pallas kernels, shards(): pl.pallas_call(layer_kernel, out_shape=jax.ShapeDtypeStruct((8, D), F32),...  128 us

profile of v6, /device:TPU:40, one launch (start us, length us, event | category | flops | bytes accessed | tf_op | source)
XLA Modules:
  0.0 129.4 jit_solution(2628052918662272272)
XLA Ops:
  0.0 127.9 %layer.1 = f32[8,4096]{1,0:T(8,128)} custom-call(bf16[1024,4096]{1,0:T(8,128)(2,1)} %prefix.1, bf16[8,4096]{1,0:T(8,128)(2,1)} %latent.1, s32[1,256]{1,0:T(1,128)} %bitcast.7, f32[1,4096]{1,0:T(1,128)} %bitcast.4, f32[1,4096]{1,0:T(1,128)} %bitcast.5, f32[1,4096]{1,0:T(1,128)} %bitcast.6, bf16[512,128]{1,0:T(8,128)(2,1)} %cq.1, bf16[512,128]{1,0:T(8,128)(2,1)} %ck.1, ...), custom_call_target="tpu_custom_call" | custom-call | tf_op jit(solution)/shard_map/layer/pallas_call | solution.py:627
  127.9 1.6 %copy.20 = f32[8,4096]{1,0:T(8,128)} copy(f32[8,4096]{1,0:T(8,128)} %layer.1) | data formatting | bytes 262144

commit v7 on v6

--- a/solution.py
+++ b/solution.py
@@ -301,10 +301,10 @@
     gather_step(0, 4)
     norm_prefix(6)
     spread_cross(3, (2, 3))
-    norm_prefix(7)
     pltpu.make_async_copy(raw_o, raw_o, ls.at[5]).wait()
     wo[b] = perturbed(raw_o[0], raw_o[1])
     spread_wo(0)
+    norm_prefix(7)
     spread_cross(4, (0, 1, 2, 3))
     prefix_part(yl, True)
     gather_end(0, range(8))
@@ -401,9 +401,9 @@
     spread_wo(2)
     arrived(lim.at[pl.ds(1, 7)], S_LIM)
     lax.fori_loop(0, 4, attend_partner_row, 0)
-    lax.fori_loop(0, 3, attend_own_row, 0)
+    lax.fori_loop(0, 1, attend_own_row, 0)
     spread_wo(3)
-    lax.fori_loop(3, 4, attend_own_row, 0)
+    lax.fori_loop(1, 4, attend_own_row, 0)
     orx[0] = otx[0]
     strx[0] = sttx[0]
     for i in range(1, 4):
@@ -505,11 +505,13 @@
 
     near, far = (0, 1, 7, 2, 6), (3, 5, 4)
     gather_step(1, 1)
+    spread_so(1)
     gather_step(1, 2)
-    spread_so(1)
+    spread_so(2)
     gather_step(1, 3)
     spread_self(4)
     spread_self(5)
+    spread_so(3)
     gather_end(1, near)
     keyval(near, 0)
     spread_keyval(0, (0, 1))
@@ -518,7 +520,6 @@
     keyval(far, 160)
     spread_keyval(0, (2, 3))
     spread_keyval(1, (0, 1))
-    spread_so(2)
     queries = natural(dot(latent_rows(1), sqkv[:, :, :HD].reshape(D, HD)), HD).astype(BF16)
 
     def absorb(source, own):
@@ -555,7 +556,6 @@
     spread_keyval(1, (2, 3))
     spread_keyval(3, (0, 1))
     spread_keyval(2, (2, 3))
-    spread_so(3)
     spread_keyval(3, (2, 3))
     spread_keyval(4, range(4))
     absorb_earlier(1, 3, 2)

time: 130 us -> 128 us (0.985)
  Pallas kernels: 128 us -> 125 us
    pallas_call x1, Pallas kernels: 128 us -> 125 us  [shards(): pl.pallas_call(layer_kernel, out_shape=jax.ShapeDtypeStruct((8, D), F32),...]
where the time goes in v7:
time: 128 us; the launch traced here: 127 us
  Pallas kernels  125 us (98%)
  local copies, waits for them, and re-layouts  1.57 us (1%)
    pallas_call x1, Pallas kernels, shards(): pl.pallas_call(layer_kernel, out_shape=jax.ShapeDtypeStruct((8, D), F32),...  125 us

profile of v7, /device:TPU:40, one launch (start us, length us, event | category | flops | bytes accessed | tf_op | source)
XLA Modules:
  0.0 127.0 jit_solution(10631884814306652964)
XLA Ops:
  0.0 125.4 %layer.1 = f32[8,4096]{1,0:T(8,128)} custom-call(bf16[1024,4096]{1,0:T(8,128)(2,1)} %prefix.1, bf16[8,4096]{1,0:T(8,128)(2,1)} %latent.1, s32[1,256]{1,0:T(1,128)} %bitcast.7, f32[1,4096]{1,0:T(1,128)} %bitcast.4, f32[1,4096]{1,0:T(1,128)} %bitcast.5, f32[1,4096]{1,0:T(1,128)} %bitcast.6, bf16[512,128]{1,0:T(8,128)(2,1)} %cq.1, bf16[512,128]{1,0:T(8,128)(2,1)} %ck.1, ...), custom_call_target="tpu_custom_call" | custom-call | tf_op jit(solution)/shard_map/layer/pallas_call | solution.py:627
  125.4 1.6 %copy.20 = f32[8,4096]{1,0:T(8,128)} copy(f32[8,4096]{1,0:T(8,128)} %layer.1) | data formatting | bytes 262144
